TPU v7x, 128 devices: a whole 4x4x4 slice. The times are simulated.
128 devices in a mesh: row: 16 (over y, x), col: 8 (over z, core).
Axes of the slice: x: 4, y: 4, z: 4, core: 2. Of those that a mesh axis runs over, the one named last changes fastest.
Arguments:
- basis_values: bfloat16 [196608, 2048], P(('row', 'col')), may hold values from -6 to 6
- point_weights: float32 [196608], P(('row', 'col')), may hold values from 0.005 to 0.05
- density_stored: bfloat16 [16384, 16384], P('row', 'col'), may hold values from -0.0029907227 to 0.0029907227
- relevant_blocks: int32 [128, 16], replicated, may hold values from 0 to 127, as said below
- relevant_count: int32 [128], replicated, may hold values from 8 to 16, as said below
- block_home: int32 [128], replicated, may hold values from 0 to 127, as said below
Outputs:
- potential_matrix: float32 [16384, 16384], P('row', 'col')
Inputs may be any that keep to these rules, and one draw needn't show every extreme that they name: `relevant_blocks`: A group's list, in order, names blocks whose stored positions are s, s + 1, s + 2, ... modulo 128 for some start s of that group, over all 16 entries; only the first relevant_count[d] are live. So a group's live entries fall at most 1 to one residue class modulo 16 and at most 2 to one modulo 8, and some group reaches both in every draw. `relevant_count`: some group has 16 live entries and some has 8. `block_home`: A permutation of the stored positions.
All inputs are finite; a program needn't handle non-finite values.
Results may differ from a plain program's by a relative error of at most 0.0029.
Values may be sent and summed in bfloat16 or wider, within the bound.
A program may use at most 128 MiB of HBM per device.

v0:
```python
import jax
import jax.numpy as jnp
from jax import lax
from jax.sharding import PartitionSpec as P


def choose_slots(residues, live, classes, capacity):
    class_ids = jnp.arange(classes, dtype=jnp.int32)
    match = (residues[:, None, :] == class_ids[None, :, None]) & live[:, None, :]
    order = jnp.cumsum(match.astype(jnp.int32), axis=2) - 1
    slot_ids = jnp.arange(capacity, dtype=jnp.int32)
    chosen = match[:, :, None, :] & (order[:, :, None, :] == slot_ids[None, None, :, None])
    entry_ids = jnp.arange(residues.shape[1], dtype=jnp.int32)
    picked = jnp.sum(jnp.where(chosen, entry_ids, 0), axis=3)
    present = jnp.any(chosen, axis=3)
    standing = jnp.sum(jnp.where(match, order, 0), axis=1)
    return (picked, present, standing)


def body(basis_values, point_weights, density_stored, relevant_blocks, relevant_count, block_home):
    row_count = lax.axis_size("row")
    col_count = lax.axis_size("col")
    groups = row_count * col_count
    own_row = lax.axis_index("row")
    own_col = lax.axis_index("col")
    own_group = own_row * col_count + own_col
    entry_limit = relevant_blocks.shape[1]
    full_width = basis_values.shape[1]
    functions_per_block = full_width // entry_limit
    block_rows = density_stored.shape[0] // functions_per_block
    block_cols = density_stored.shape[1] // functions_per_block
    cap_rows = entry_limit // row_count
    cap_cols = entry_limit // col_count
    positions = block_home[relevant_blocks]
    live = jnp.arange(entry_limit, dtype=jnp.int32)[None, :] < relevant_count[:, None]
    row_pick, row_present, row_rank = choose_slots(positions % row_count, live, row_count, cap_rows)
    col_pick, col_present, col_rank = choose_slots(positions % col_count, live, col_count, cap_cols)
    owned_rpick = lax.dynamic_index_in_dim(row_pick, own_row, 1, keepdims=False)
    owned_rkeep = lax.dynamic_index_in_dim(row_present, own_row, 1, keepdims=False)
    owned_cpick = lax.dynamic_index_in_dim(col_pick, own_col, 1, keepdims=False)
    owned_ckeep = lax.dynamic_index_in_dim(col_present, own_col, 1, keepdims=False)
    local_rows = jnp.take_along_axis(positions, owned_rpick, axis=1) // row_count
    local_cols = jnp.take_along_axis(positions, owned_cpick, axis=1) // col_count
    keep_slot = owned_rkeep[:, :, None] & owned_ckeep[:, None, :]
    stored = density_stored.reshape(
        block_rows, functions_per_block, block_cols, functions_per_block
    ).transpose(0, 2, 1, 3)
    outgoing = stored[local_rows[:, :, None], local_cols[:, None, :]]
    outgoing = jnp.where(keep_slot[:, :, :, None, None], outgoing, jnp.zeros((), outgoing.dtype))
    incoming = lax.all_to_all(outgoing, ("row", "col"), split_axis=0, concat_axis=0, tiled=True)
    incoming = incoming.reshape(
        row_count, col_count, cap_rows, cap_cols, functions_per_block, functions_per_block
    )
    own_pos = lax.dynamic_index_in_dim(positions, own_group, 0, keepdims=False)
    own_live = lax.dynamic_index_in_dim(live, own_group, 0, keepdims=False)
    own_rrank = jnp.clip(
        lax.dynamic_index_in_dim(row_rank, own_group, 0, keepdims=False), 0, cap_rows - 1
    )
    own_crank = jnp.clip(
        lax.dynamic_index_in_dim(col_rank, own_group, 0, keepdims=False), 0, cap_cols - 1
    )
    sub = incoming[
        (own_pos % row_count)[:, None],
        (own_pos % col_count)[None, :],
        own_rrank[:, None],
        own_crank[None, :],
    ]
    sub = sub.transpose(0, 2, 1, 3).reshape(full_width, full_width)
    columns_live = jnp.repeat(own_live, functions_per_block)
    orbital_values = jnp.where(
        columns_live[None, :], basis_values, jnp.zeros((), basis_values.dtype)
    )
    dens = jnp.dot(orbital_values, sub, preferred_element_type=jnp.float32)
    rho = jnp.sum(dens * orbital_values.astype(jnp.float32), axis=1)
    pot = point_weights * rho * (1.0 + rho * rho) ** (-1.0 / 3.0)
    weighted_orbitals = (orbital_values.astype(jnp.float32) * pot[:, None]).astype(jnp.bfloat16)
    potential_submatrix = jnp.dot(
        orbital_values.T, weighted_orbitals, preferred_element_type=jnp.float32
    )
    potential_blocks = potential_submatrix.reshape(
        entry_limit, functions_per_block, entry_limit, functions_per_block
    ).transpose(0, 2, 1, 3)
    send_rpick = lax.dynamic_index_in_dim(row_pick, own_group, 0, keepdims=False)
    send_rkeep = lax.dynamic_index_in_dim(row_present, own_group, 0, keepdims=False)
    send_cpick = lax.dynamic_index_in_dim(col_pick, own_group, 0, keepdims=False)
    send_ckeep = lax.dynamic_index_in_dim(col_present, own_group, 0, keepdims=False)
    partial_value = potential_blocks[send_rpick[:, None, :, None], send_cpick[None, :, None, :]]
    partial_keep = send_rkeep[:, None, :, None] & send_ckeep[None, :, None, :]
    partial_value = jnp.where(
        partial_keep[:, :, :, :, None, None], partial_value, jnp.zeros((), jnp.float32)
    )
    returned = lax.all_to_all(
        partial_value.reshape(groups, cap_rows, cap_cols, functions_per_block, functions_per_block),
        ("row", "col"),
        split_axis=0,
        concat_axis=0,
        tiled=True,
    )
    total = jnp.zeros(
        (block_rows, block_cols, functions_per_block, functions_per_block), jnp.float32
    )
    total = total.at[local_rows[:, :, None], local_cols[:, None, :]].add(returned)
    return total.transpose(0, 2, 1, 3).reshape(
        block_rows * functions_per_block, block_cols * functions_per_block
    )


def solution(mesh):
    in_specs = (P(("row", "col"), None), P(("row", "col")), P("row", "col"), P(), P(), P())
    out_specs = P("row", "col")
    return jax.shard_map(body, mesh=mesh, in_specs=in_specs, out_specs=out_specs, check_vma=False)
```

profile of v0, /device:TPU:42, one launch (start us, length us, event | category | flops | bytes accessed | tf_op | source)
XLA Modules:
  0.0 580.3 jit_solution(16313399773317747724)
XLA Ops:
  0.0 0.0 copy-start
  0.0 0.7 compare_select_fusion.2
  0.7 0.1 copy.168
  0.8 0.1 reshape.393
  0.9 0.0 copy-done
  0.9 0.0 copy-start.3
  0.9 12.6 %gather_fusion = s32[2048]{0:T(1024)S(1)} fusion(s32[128]{0:T(128)S(1)} %copy-done, s32[2048]{0:T(1024)S(1)} %broadcast_clamp_fusion), kind=kCustom, calls=%fused_computation | custom fusion | bytes 24576 | tf_op jit(solution)/shard_map/gather | solution.py:34
  13.6 0.1 reshape.392
  13.6 0.1 copy.169
  13.7 0.0 copy-done.3
  13.9 0.1 select_reduce_fusion.1
  14.0 0.1 copy.174
  14.1 0.1 reshape.429
  14.3 1.9 gather_fusion.5
  16.2 0.1 gather.30
  16.4 0.1 copy.175
  16.5 0.1 fusion.46
  16.6 1.3 gather_fusion.4
  18.0 0.1 copy.181
  18.1 0.1 reshape.401
  18.2 3.6 copy.190
  21.8 3.1 copy.203
  24.9 0.1 copy.179
  25.1 12.3 %gather_fusion.1 = bf16[256,128,128]{2,1,0:T(8,128)(2,1)} fusion(bf16[8,16,128,128]{3,2,1,0:T(8,128)(2,1)} %bitcast.79, s32[256]{0:T(256)S(1)} %reshape.401), kind=kCustom, calls=%fused_computation.1 | custom fusion | bytes 16779264 | tf_op jit(solution)/shard_map/gather | solution.py:48
  37.3 7.4 %broadcast_select_fusion.1 = bf16[128,1,2,128,128]{4,3,2,1,0:T(8,128)(2,1)} fusion(bf16[128,1,2,128,128]{4,3,2,1,0:T(8,128)(2,1)} %bitcast.80, pred[128,2]{1,0:T(8,128)(4,1)S(1)} %copy.179), kind=kLoop, calls=%fused_computation.18 | loop fusion | flops 4194304 | bytes 16777472 | tf_op jit(solution)/shard_map/jit(_where)/select_n | solution.py:49
  44.8 11.0 %all-to-all-start = ((bf16[128,1,2,128,128]{4,3,2,1,0:T(8,128)(2,1)}), bf16[128,1,2,128,128]{4,3,2,1,0:T(8,128)(2,1)}, u32[]{:S(2)}, u32[]{:S(2)}) async-start(bf16[128,1,2,128,128]{4,3,2,1,0:T(8,128)(2,1)} %broadcast_select_fusion.1), calls=%async_computation | async-start | bytes 16777216 | tf_op jit(solution)/shard_map/all_to_all | solution.py:50
  55.8 0.2 dynamic-slice_reduce_fusion
  56.0 0.2 fusion.28
  56.2 0.2 dynamic-slice_reduce_fusion.3
  56.4 0.1 or_or_fusion
  56.5 0.1 reshape.407
  56.6 0.1 constant_dynamic-slice_fusion
  56.7 0.1 copy.186
  56.8 0.1 broadcast_in_dim.184
  56.9 0.1 copy.187
  57.0 0.1 reshape.415
  57.2 0.1 constant_dynamic-slice_fusion.3
  57.2 0.1 copy.177
  57.4 0.1 copy.178
  57.5 0.2 dynamic-slice_reduce_fusion.1
  57.6 0.1 and.186
  57.7 0.1 and.187
  57.8 0.1 broadcast_bitcast_fusion
  57.9 0.1 bitcast_and_fusion
  58.0 97.4 %all-to-all-done = bf16[128,1,2,128,128]{4,3,2,1,0:T(8,128)(2,1)} async-done(((bf16[128,1,2,128,128]{4,3,2,1,0:T(8,128)(2,1)}), bf16[128,1,2,128,128]{4,3,2,1,0:T(8,128)(2,1)}, u32[]{:S(2)}, u32[]{:S(2)}) %all-to-all-start) | async-done | bytes 8388640 | tf_op jit(solution)/shard_map/all_to_all | solution.py:50
  155.4 9.4 %gather_fusion.2 = bf16[256,128,128]{2,1,0:T(8,128)(2,1)} fusion(bf16[16,8,1,2,128,128]{5,4,3,2,1,0:T(8,128)(2,1)} %bitcast.15, s32[256]{0:T(256)S(1)} %reshape.407), kind=kCustom, calls=%fused_computation.2 | custom fusion | bytes 16781312 | tf_op jit(solution)/shard_map/gather | solution.py:62
  164.8 13.8 %copy.184 = bf16[16,16,128,128]{3,1,2,0:T(8,128)(2,1)} copy(bf16[16,16,128,128]{3,2,1,0:T(8,128)(2,1)} %bitcast.81) | data formatting | bytes 16777216 | tf_op jit(solution)/shard_map/gather | solution.py:62
  178.6 18.9 %fusion = f32[1536]{0:T(1024)S(1)} fusion(bf16[256,8,16,128]{3,2,1,0:T(8,128)(2,1)} %bitcast.84, bf16[1536,2048]{1,0:T(8,128)(2,1)} %param.6, pred[2048]{0:T(1024)(128)(4,1)S(1)} %broadcast_bitcast_fusion), kind=kOutput, calls=%fused_computation.10 | convolution fusion | flops 12900628480 | bytes 14688256 | tf_op jit(solution)/shard_map/dot_general | solution.py:73
  197.5 0.0 copy-done.2
  197.6 0.0 slice-done
  197.6 16.9 %fusion.4 = f32[256,8,16,128]{3,1,2,0:T(8,128)} fusion(f32[1536]{0:T(1024)S(1)} %power_multiply_fusion, bf16[1536,2048]{1,0:T(8,128)(2,1)S(1)} %bitcast.88, pred[2048]{0:T(1024)(128)(4,1)S(1)} %broadcast_bitcast_fusion), kind=kOutput, calls=%fused_computation.13 | convolution fusion | flops 12900630528 | bytes 23076864 | tf_op jit(solution)/shard_map/dot_general | solution.py:77
  214.5 9.4 %copy.192 = f32[256,8,16,128]{3,2,1,0:T(8,128)S(1)} copy(f32[256,8,16,128]{3,1,2,0:T(8,128)} %fusion.4) | data formatting | bytes 33554432
  223.9 7.8 %copy.201 = f32[16,128,16,128]{3,1,2,0:T(8,128)} copy(f32[16,128,16,128]{3,2,1,0:T(8,128)S(1)} %bitcast.77) | data formatting | bytes 33554432 | tf_op jit(solution)/shard_map/reshape | solution.py:80
  231.7 18.9 %gather_fusion.3 = f32[256,128,128]{2,1,0:T(8,128)} fusion(f32[16,16,128,128]{3,2,1,0:T(8,128)} %bitcast.76, s32[256]{0:T(256)S(1)} %reshape.415), kind=kCustom, calls=%fused_computation.3 | custom fusion | bytes 33556480 | tf_op jit(solution)/shard_map/gather | solution.py:87
  250.6 11.4 %broadcast_select_fusion = f32[128,1,2,128,128]{4,3,2,1,0:T(8,128)} fusion(f32[128,1,2,128,128]{4,3,2,1,0:T(8,128)} %bitcast.78, pred[128,2]{1,0:T(8,128)(4,1)S(1)} %bitcast_and_fusion), kind=kLoop, calls=%fused_computation.17 | loop fusion | flops 4194304 | bytes 33554688 | tf_op jit(solution)/shard_map/jit(_where)/select_n | solution.py:89
  262.0 12.2 %all-to-all-start.1 = ((f32[128,1,2,128,128]{4,3,2,1,0:T(8,128)}), f32[128,1,2,128,128]{4,3,2,1,0:T(8,128)}, u32[]{:S(2)}, u32[]{:S(2)}) async-start(f32[128,1,2,128,128]{4,3,2,1,0:T(8,128)} %broadcast_select_fusion), calls=%async_computation.1 | async-start | bytes 33554432 | tf_op jit(solution)/shard_map/all_to_all | solution.py:92
  274.2 0.1 copy.176
  274.3 0.1 reshape.437
  274.4 233.1 %all-to-all-done.1 = f32[128,1,2,128,128]{4,3,2,1,0:T(8,128)} async-done(((f32[128,1,2,128,128]{4,3,2,1,0:T(8,128)}), f32[128,1,2,128,128]{4,3,2,1,0:T(8,128)}, u32[]{:S(2)}, u32[]{:S(2)}) %all-to-all-start.1) | async-done | bytes 16777248 | tf_op jit(solution)/shard_map/all_to_all | solution.py:92
  507.6 4.5 broadcast_in_dim.98
  512.0 52.2 %scatter_fusion = f32[8,16,128,128]{3,2,1,0:T(8,128)} fusion(f32[8,16,128,128]{3,2,1,0:T(8,128)} %broadcast_in_dim.98, s32[256]{0:T(256)S(1)} %reshape.437, f32[256,128,128]{2,1,0:T(8,128)} %bitcast.23), kind=kCustom, calls=%fused_computation.6 | custom fusion | flops 4194304 | bytes 50333696 | tf_op jit(solution)/shard_map/scatter-add | solution.py:102
  564.3 8.1 %copy.189 = f32[8,128,16,128]{3,2,1,0:T(8,128)S(1)} copy(f32[8,128,16,128]{3,1,2,0:T(8,128)} %bitcast.75) | data formatting | bytes 16777216 | tf_op jit(solution)/shard_map/transpose | solution.py:103
  572.4 0.0 copy-start.1
  572.4 7.5 %copy.202 = f32[128,8,16,128]{3,1,2,0:T(8,128)} copy(f32[128,8,16,128]{3,2,1,0:T(8,128)S(1)} %bitcast.82) | data formatting | bytes 16777216
  (34 shorter events, 0.5 us)
Async XLA Ops:
  0.0 0.9 copy-start
  0.9 12.8 %copy-start.3 = (s32[128]{0:T(128)S(1)}, s32[128]{0:T(128)}, u32[]{:S(2)}) copy-start(s32[128]{0:T(128)} %param.10) | copy-start | bytes 1540
  44.8 110.6 %all-to-all-start = ((bf16[128,1,2,128,128]{4,3,2,1,0:T(8,128)(2,1)}), bf16[128,1,2,128,128]{4,3,2,1,0:T(8,128)(2,1)}, u32[]{:S(2)}, u32[]{:S(2)}) async-start(bf16[128,1,2,128,128]{4,3,2,1,0:T(8,128)(2,1)} %broadcast_select_fusion.1), calls=%async_computation | async-start | bytes 16777216 | tf_op jit(solution)/shard_map/all_to_all | solution.py:50
  164.8 32.8 %slice-start = ((s8[6291456]{0:T(1024)(128)(4,1)}), s8[2097152]{0:T(1024)(128)(4,1)S(1)}, s32[]{:S(2)}) async-start(s8[6291456]{0:T(1024)(128)(4,1)} %bitcast.87), calls=%async_computation.2 | async-start | bytes 4194304
  178.6 18.9 %copy-start.2 = (f32[1536]{0:T(1024)S(1)}, f32[1536]{0:T(1024)}, u32[]{:S(2)}) copy-start(f32[1536]{0:T(1024)} %param.7) | copy-start | bytes 18436
  178.6 18.9 %slice-start.1 = ((s8[6291456]{0:T(1024)(128)(4,1)}), s8[4194304]{0:T(1024)(128)(4,1)S(1)}, s32[]{:S(2)}) async-start(s8[6291456]{0:T(1024)(128)(4,1)} %bitcast.87), calls=%async_computation.3 | async-start | bytes 8388608
  262.0 245.6 %all-to-all-start.1 = ((f32[128,1,2,128,128]{4,3,2,1,0:T(8,128)}), f32[128,1,2,128,128]{4,3,2,1,0:T(8,128)}, u32[]{:S(2)}, u32[]{:S(2)}) async-start(f32[128,1,2,128,128]{4,3,2,1,0:T(8,128)} %broadcast_select_fusion), calls=%async_computation.1 | async-start | bytes 33554432 | tf_op jit(solution)/shard_map/all_to_all | solution.py:92
  572.4 7.5 %copy-start.1 = (s32[128]{0:T(128)S(1)}, s32[128]{0:T(128)}, u32[]{:S(2)}) copy-start(s32[128]{0:T(128)} %param.11) | copy-start | bytes 1540
where the time goes:
time: 588 us; the launch traced here: 580 us
  waiting for transfers between devices  331 us (56%)
  local copies, waits for them, and re-layouts  117 us (20%)
  other arithmetic  72.8 us (12%)
  matrix products  35.8 us (6%)
  starting transfers between devices  23.2 us (4%)
    all_to_all x1, waiting for transfers between devices, body(): lax.all_to_all(partial_value.reshape(groups, cap_rows, cap_cols, function...  233 us
    all_to_all x1, waiting for transfers between devices, body(): lax.all_to_all(outgoing, ('row', 'col'), split_axis=0, concat_axis=0, til...  97.4 us
    scatter-add x1, other arithmetic, body(): total.at[local_rows[:, :, None], local_cols[:, None, :]].add(returned)  52.2 us
    gather x2, local copies, waits for them, and re-layouts, body(): incoming[(own_pos % row_count)[:, None], (own_pos % col_count)[None, :],...  23.2 us
    unnamed x16, local copies, waits for them, and re-layouts  20.5 us
    gather x1, local copies, waits for them, and re-layouts, body(): potential_blocks[send_rpick[:, None, :, None], send_cpick[None, :, None, :]]  18.9 us
    dot_general x1, matrix products, body(): dens = jnp.dot(orbital_values, sub, preferred_element_type=jnp.float32)  18.9 us
    dot_general x1, matrix products, body(): jnp.dot(orbital_values.T, weighted_orbitals, preferred_element_type=jnp.f...  16.9 us
  transfers between devices with their start and end apart: 2, of which 2 were waited for; matrix products, arithmetic and copies ran while one was open for 0% of the time, Pallas kernels for 0%

commit v1 on v0

v1 whole, which is shorter than its diff:
```python
import functools

import jax
import jax.numpy as jnp
from jax import lax
from jax.experimental import pallas as pl
from jax.experimental.pallas import tpu as pltpu
from jax.sharding import PartitionSpec as P

MESH = pl.DeviceIdType.MESH
NROW, NCOL, GROUPS, B = 16, 8, 128, 128
ENTRIES = 16
ROWS = 1536
WIDTH = ENTRIES * B


def place(residue):
    return (residue % NCOL) * 2 + residue // NCOL


def offset_target(step, row, col):
    t = (step * (step + 1) // 2) % GROUPS
    y = (row // 4 + t % 4) % 4
    x = (row % 4 + (t // 4) % 4) % 4
    z = (col // 2 + (t // 16) % 4) % 4
    core = (col + t // 64) % 2
    return y * 4 + x, z * 2 + core


def position(start, residue, period):
    return (start + ((residue - start) & (ENTRIES - 1))) & (GROUPS - 1)


def group_kernel(
    start_ref, cnt_ref, w_ref, dens_hbm, phi_hbm, out_ref,
    dens_ref, phi_ref, scaled_ref, phit_ref, sub_ref, stage_ref, rho_ref, pot_ref,
    dens_sem, phi_sem, dsend, drecv, vsend, vrecv, self_sem,
):
    row, col = lax.axis_index("row"), lax.axis_index("col")
    me = row * NCOL + col

    def column(k):
        return pl.ds(k * B, B)

    dens_copies = [
        pltpu.make_async_copy(dens_hbm.at[:, :, column(k)], dens_ref.at[k], dens_sem) for k in range(ENTRIES)
    ]
    phi_copies = [
        pltpu.make_async_copy(phi_hbm.at[:, column(k)], phi_ref.at[k], phi_sem) for k in range(ENTRIES)
    ]
    for copy in dens_copies + phi_copies:
        copy.start()

    barrier = pltpu.get_barrier_semaphore()

    def greet(i, carry):
        r, c = offset_target(i, row, col)
        pl.semaphore_signal(barrier, inc=1, device_id=(r, c), device_id_type=MESH)
        return carry

    lax.fori_loop(1, GROUPS, greet, 0)

    def pick(r, c):
        start = start_ref[r * NCOL + c]
        i = position(start, row, NROW) >> 4
        j0 = position(start, col, ENTRIES) >> 3
        j1 = position(start, col + NCOL, ENTRIES) >> 3
        return dens_ref[j0, i], dens_ref[j1, i]

    def slot(r, c):
        return pl.multiple_of((c * ENTRIES + place(r)) * B, B)

    pltpu.make_async_copy(dens_ref, dens_ref, dens_sem).wait()

    def prepare(i, carry):
        r, c = offset_target(i, row, col)
        left, right = pick(r, c)
        at = slot(r, c)
        stage_ref[pl.ds(at, B), pl.ds(0, B)] = left
        stage_ref[pl.ds(at, B), pl.ds(B, B)] = right
        return carry

    lax.fori_loop(1, GROUPS, prepare, 0)
    my_rows = pl.ds(pl.multiple_of(place(row) * B, B), B)
    my_cols = pl.ds(pl.multiple_of(col * 2 * B, B), 2 * B)
    left, right = pick(row, col)
    sub_ref[my_rows, my_cols] = jnp.concatenate([left, right], axis=1)

    pl.semaphore_wait(barrier, GROUPS - 1)

    def send(i, carry):
        r, c = offset_target(i, row, col)
        pltpu.make_async_remote_copy(
            src_ref=stage_ref.at[pl.ds(slot(r, c), B)],
            dst_ref=sub_ref.at[my_rows, my_cols],
            send_sem=dsend, recv_sem=drecv,
            device_id=(r, c), device_id_type=MESH,
        ).start()
        return carry

    lax.fori_loop(1, GROUPS, send, 0)

    pltpu.make_async_copy(phi_ref, phi_ref, phi_sem).wait()
    my_start = start_ref[me]
    my_count = cnt_ref[me]

    def turn(at, carry):
        residue = at // 2 + (at % 2) * NCOL
        k = (residue - my_start) & (ENTRIES - 1)
        live = jnp.clip(my_count - k, 0, 1).astype(jnp.float32)
        for t in range(ROWS // B):
            tile = phi_ref[k, pl.ds(t * B, B), :]
            tile = (tile.astype(jnp.float32) * live).T
            phit_ref[pl.ds(pl.multiple_of(at * B, B), B), pl.ds(t * B, B)] = tile.astype(jnp.bfloat16)
        return carry

    lax.fori_loop(0, ENTRIES, turn, 0)
    rho_ref[...] = jnp.zeros_like(rho_ref)

    everything = stage_ref.at[pl.ds(0, (GROUPS - 1) * B)]
    pltpu.make_async_copy(everything, everything, drecv).wait()

    M, N = 512, 256

    def density(step, carry):
        rows = pl.ds(pl.multiple_of((step % (WIDTH // M)) * M, M), M)
        cols = pl.ds(pl.multiple_of((step // (WIDTH // M)) * N, N), N)
        g = jnp.dot(sub_ref[rows, :], phit_ref[:, cols], preferred_element_type=jnp.float32)
        g = g * phit_ref[rows, cols].astype(jnp.float32)
        rho_ref[:, cols] += jnp.sum(g.reshape(M // 8, 8, N), axis=0)
        return carry

    lax.fori_loop(0, (WIDTH // M) * (ROWS // N), density, 0)

    rho = jnp.sum(rho_ref[...], axis=0, keepdims=True)
    pot_ref[...] = w_ref[...] * rho * jnp.exp(jnp.log(1.0 + rho * rho) * (-1.0 / 3.0))

    pltpu.make_async_copy(everything, everything, dsend).wait()

    def potential(i, carry):
        c = (col + i) % NCOL
        cols = pl.ds(pl.multiple_of(c * 2 * B, 2 * B), 2 * B)
        scaled_ref[...] = (
            phit_ref[cols, :].astype(jnp.float32) * pot_ref[...]
        ).astype(jnp.bfloat16)

        def part(j, carry):
            m = (row % 4 + j) % 4
            rows = pl.ds(pl.multiple_of(m * M, M), M)
            v = lax.dot_general(
                phit_ref[rows, :], scaled_ref[...],
                (((1,), (1,)), ((), ())), preferred_element_type=jnp.float32,
            )
            base = pl.multiple_of((c * ENTRIES + m * 4) * B, B)
            stage_ref[pl.ds(base, M)] = v.astype(jnp.bfloat16)
            for n in range(4):
                at = m * 4 + n
                r = at // 2 + (at % 2) * NCOL
                source = stage_ref.at[pl.ds(pl.multiple_of(base + n * B, B), B)]

                @pl.when(r * NCOL + c != me)
                def _():
                    pltpu.make_async_remote_copy(
                        src_ref=source, dst_ref=out_ref.at[me],
                        send_sem=vsend, recv_sem=vrecv,
                        device_id=(r, c), device_id_type=MESH,
                    ).start()

            return carry

        return lax.fori_loop(0, 4, part, carry)

    lax.fori_loop(0, NCOL, potential, 0)
    own = pltpu.make_async_copy(stage_ref.at[pl.ds(slot(row, col), B)], out_ref.at[me], self_sem)
    own.start()
    own.wait()
    pltpu.make_async_copy(everything, everything, vsend).wait()
    pltpu.make_async_copy(everything, everything, vrecv).wait()


def exchange(starts, cnt, w, dens, phi):
    vmem = pl.BlockSpec(memory_space=pltpu.VMEM)
    smem = pl.BlockSpec(memory_space=pltpu.SMEM)
    hbm = pl.BlockSpec(memory_space=pl.ANY)
    return pl.pallas_call(
        group_kernel,
        out_shape=jax.ShapeDtypeStruct((GROUPS, B, 2 * B), jnp.bfloat16),
        in_specs=[smem, smem, vmem, hbm, hbm],
        out_specs=hbm,
        scratch_shapes=[
            pltpu.VMEM((ENTRIES, 8, B, B), jnp.bfloat16),
            pltpu.VMEM((ENTRIES, ROWS, B), jnp.bfloat16),
            pltpu.VMEM((2 * B, ROWS), jnp.bfloat16),
            pltpu.VMEM((WIDTH, ROWS), jnp.bfloat16),
            pltpu.VMEM((WIDTH, WIDTH), jnp.bfloat16),
            pltpu.VMEM((GROUPS * B, 2 * B), jnp.bfloat16),
            pltpu.VMEM((8, ROWS), jnp.float32),
            pltpu.VMEM((1, ROWS), jnp.float32),
            pltpu.SemaphoreType.DMA,
            pltpu.SemaphoreType.DMA,
            pltpu.SemaphoreType.DMA,
            pltpu.SemaphoreType.DMA,
            pltpu.SemaphoreType.DMA,
            pltpu.SemaphoreType.DMA,
            pltpu.SemaphoreType.DMA,
        ],
        compiler_params=pltpu.CompilerParams(
            collective_id=0, has_side_effects=True, vmem_limit_bytes=56 << 20
        ),
        cost_estimate=pl.CostEstimate(flops=4 * ROWS * WIDTH * WIDTH, bytes_accessed=32 << 20, transcendentals=2 * ROWS),
    )(starts, cnt, w, dens, phi)


CHUNK = 8


def sum_kernel(where_ref, start_ref, parts_ref, out_ref):
    row, col = where_ref[0], where_ref[1]
    step = pl.program_id(0)

    @pl.when(step == 0)
    def _():
        out_ref[...] = jnp.zeros_like(out_ref)

    for n in range(CHUNK):
        start = start_ref[step * CHUNK + n]
        i = position(start, row, NROW) // NROW
        rows = pl.ds(pl.multiple_of(i * B, B), B)
        for h in range(2):
            j = position(start, col + h * NCOL, ENTRIES) // NCOL
            cols = pl.ds(pl.multiple_of(j * B, B), B)
            out_ref[rows, cols] += parts_ref[n, :, pl.ds(h * B, B)].astype(jnp.float32)


def collect(where, starts, parts):
    smem = pl.BlockSpec(memory_space=pltpu.SMEM)
    return pl.pallas_call(
        sum_kernel,
        grid=(GROUPS // CHUNK,),
        out_shape=jax.ShapeDtypeStruct((1024, WIDTH), jnp.float32),
        in_specs=[smem, smem, pl.BlockSpec((CHUNK, B, 2 * B), lambda g: (g, 0, 0))],
        out_specs=pl.BlockSpec((1024, WIDTH), lambda g: (0, 0)),
        compiler_params=pltpu.CompilerParams(vmem_limit_bytes=40 << 20),
    )(where, starts, parts)


def body(basis_values, point_weights, density_stored, relevant_blocks, relevant_count, block_home):
    starts = block_home[relevant_blocks[:, 0]]
    parts = exchange(
        starts, relevant_count, point_weights.reshape(1, ROWS), density_stored.reshape(8, B, WIDTH), basis_values,
    )
    where = jnp.stack([lax.axis_index("row"), lax.axis_index("col")]).astype(jnp.int32)
    return collect(where, starts, parts)


def solution(mesh):
    in_specs = (P(("row", "col"), None), P(("row", "col")), P("row", "col"), P(), P(), P())
    return jax.shard_map(body, mesh=mesh, in_specs=in_specs, out_specs=P("row", "col"), check_vma=False)
```

time: 588 us -> 297 us (0.51)
  the two profiles are of different devices: /device:TPU:42 before, /device:TPU:23 now
where the time goes in v1:
time: 297 us
  Pallas kernels  290 us (98%)
  local copies, waits for them, and re-layouts  6.41 us (2%)
    pallas_call x1, Pallas kernels, exchange(): pl.pallas_call(group_kernel, out_shape=jax.ShapeDtypeStruct((GROUPS, B, 2...  281 us
    pallas_call x1, Pallas kernels, collect(): pl.pallas_call(sum_kernel, grid=(GROUPS // CHUNK,), out_shape=jax.ShapeDt...  8.31 us

profile of v1, /device:TPU:23, one launch (start us, length us, event | category | flops | bytes accessed | tf_op | source)
XLA Modules:
  0.0 296.8 jit_solution(3764302066054816174)
XLA Ops:
  0.0 0.0 copy-start
  0.0 0.1 pad_add_fusion.where_ref
  0.1 0.7 fusion
  0.8 0.0 copy-done
  0.8 1.7 gather_fusion
  2.5 1.3 reshape.6.w_ref
  3.8 0.0 copy-start.2
  3.8 281.3 %shard_map.64.parts_ref = bf16[128,128,256]{2,1,0:T(8,128)(2,1)} custom-call(s32[128]{0:T(128)} %gather_fusion, s32[128]{0:T(128)} %cnt_ref.1, f32[1,1536]{1,0:T(1,128)} %reshape.6.w_ref, bf16[8,128,2048]{2,1,0:T(8,128)(2,1)} %bitcast.5, bf16[1536,2048]{1,0:T(8,128)(2,1)} %phi_hbm.1), custom_call_target="tpu_custom_call" | custom-call | flops 25769803776 | bytes 33554432 | tf_op jit(solution)/shard_map/pallas_call | solution.py:185
  285.1 0.0 copy-done.2
  285.1 0.0 copy-start.1
  285.2 3.4 %copy-done.1 = bf16[128,128,256]{2,1,0:T(8,128)(2,1)S(1)} copy-done((bf16[128,128,256]{2,1,0:T(8,128)(2,1)S(1)}, bf16[128,128,256]{2,1,0:T(8,128)(2,1)}, u32[]{:S(2)}) %copy-start.1) | copy-done | bytes 8388632
  288.5 8.3 %shard_map.65 = f32[1024,2048]{1,0:T(8,128)} custom-call(s32[2]{0:T(128)S(1)} %pad_add_fusion.where_ref, s32[128]{0:T(128)S(1)} %copy-done.2, bf16[128,128,256]{2,1,0:T(8,128)(2,1)S(1)} %copy-done.1), custom_call_target="tpu_custom_call" | custom-call | tf_op jit(solution)/shard_map/pallas_call | solution.py:237
  (1 shorter events, 0.0 us)
Async XLA Ops:
  0.0 0.8 copy-start
  3.8 281.3 %copy-start.2 = (s32[128]{0:T(128)S(1)}, s32[128]{0:T(128)}, u32[]{:S(2)}) copy-start(s32[128]{0:T(128)} %gather_fusion) | copy-start | bytes 1540
  285.1 3.4 %copy-start.1 = (bf16[128,128,256]{2,1,0:T(8,128)(2,1)S(1)}, bf16[128,128,256]{2,1,0:T(8,128)(2,1)}, u32[]{:S(2)}) copy-start(bf16[128,128,256]{2,1,0:T(8,128)(2,1)} %shard_map.64.parts_ref) | copy-start | bytes 25165828

commit v2 on v1

v2 whole, which is shorter than its diff:
```python
import jax
import jax.numpy as jnp
from jax import lax
from jax.experimental import pallas as pl
from jax.experimental.pallas import tpu as pltpu
from jax.sharding import PartitionSpec as P

MESH = pl.DeviceIdType.MESH
NROW, NCOL, GROUPS, B = 16, 8, 128, 128
ENTRIES = 16
ROWS = 1536
WIDTH = ENTRIES * B
BLOCK_ROWS = 8
GATHER_ROUNDS, GATHER_ROWS = 4, 32
RETURN_ROUNDS, RETURN_ROWS = 2, 64


def place(residue):
    return (residue % NCOL) * 2 + residue // NCOL


def offset_target(step, row, col):
    t = (step * (step + 1) // 2) % GROUPS
    y = (row // 4 + t % 4) % 4
    x = (row % 4 + (t // 4) % 4) % 4
    z = (col // 2 + (t // 16) % 4) % 4
    core = (col + t // 64) % 2
    return y * 4 + x, z * 2 + core


def list_place(start, residue):
    return (residue - start) & (ENTRIES - 1)


def position(start, residue):
    return (start + list_place(start, residue)) & (GROUPS - 1)


def lag(row, col):
    return (col - row + NROW) % NCOL


def group_kernel(
    start_ref, cnt_ref, w_ref, dens_hbm, phi_hbm, main_ref, far_ref,
    dens_ref, phi_ref, scaled_ref, phit_ref, sub_ref, stage_ref, back_ref, rho_ref, pot_ref,
    dens_sem, phi_sem, dsend, drecv, msend, mrecv, fsend, frecv, self_sem,
):
    row, col = lax.axis_index("row"), lax.axis_index("col")
    me = row * NCOL + col

    def column(k):
        return pl.ds(k * B, B)

    dens_copies = [
        pltpu.make_async_copy(dens_hbm.at[:, :, column(k)], dens_ref.at[k], dens_sem) for k in range(ENTRIES)
    ]
    phi_copies = [
        pltpu.make_async_copy(phi_hbm.at[:, column(k)], phi_ref.at[k], phi_sem) for k in range(ENTRIES)
    ]
    for copy in dens_copies + phi_copies:
        copy.start()

    barrier = pltpu.get_barrier_semaphore()

    def greet(i, carry):
        r, c = offset_target(i, row, col)
        pl.semaphore_signal(barrier, inc=1, device_id=(r, c), device_id_type=MESH)
        return carry

    lax.fori_loop(1, GROUPS, greet, 0)

    def pick(r, c):
        start = start_ref[r * NCOL + c]
        i = position(start, row) >> 4
        j0 = position(start, col) >> 3
        j1 = position(start, col + NCOL) >> 3
        return dens_ref[j0, i], dens_ref[j1, i]

    pltpu.make_async_copy(dens_ref, dens_ref, dens_sem).wait()

    def staged(n, r, c):
        at = (n * GROUPS + r * NCOL + c) * GATHER_ROWS
        return pl.ds(pl.multiple_of(at, GATHER_ROWS), GATHER_ROWS)

    def prepare(i, carry):
        r, c = offset_target(i, row, col)
        left, right = pick(r, c)
        for n in range(GATHER_ROUNDS):
            part = slice(n * GATHER_ROWS, (n + 1) * GATHER_ROWS)
            stage_ref[staged(n, r, c), pl.ds(0, B)] = left[part]
            stage_ref[staged(n, r, c), pl.ds(B, B)] = right[part]
        return carry

    lax.fori_loop(1, GROUPS, prepare, 0)
    my_rows = pl.ds(pl.multiple_of(place(row) * GATHER_ROWS, GATHER_ROWS), GATHER_ROWS)
    my_cols = pl.ds(pl.multiple_of(col * 2 * B, B), 2 * B)
    left, right = pick(row, col)
    for n in range(GATHER_ROUNDS):
        part = slice(n * GATHER_ROWS, (n + 1) * GATHER_ROWS)
        sub_ref[n, my_rows, my_cols] = jnp.concatenate([left[part], right[part]], axis=1)

    pl.semaphore_wait(barrier, GROUPS - 1)

    def send_round(n, carry):
        def send(i, carry):
            r, c = offset_target(i, row, col)
            pltpu.make_async_remote_copy(
                src_ref=stage_ref.at[staged(n, r, c)],
                dst_ref=sub_ref.at[n, my_rows, my_cols],
                send_sem=dsend, recv_sem=drecv.at[n],
                device_id=(r, c), device_id_type=MESH,
            ).start()
            return carry

        return lax.fori_loop(1, GROUPS, send, carry)

    lax.fori_loop(0, GATHER_ROUNDS, send_round, 0)

    pltpu.make_async_copy(phi_ref, phi_ref, phi_sem).wait()
    my_start = start_ref[me]
    my_count = cnt_ref[me]

    def turn(at, carry):
        residue = at // 2 + (at % 2) * NCOL
        k = list_place(my_start, residue)
        live = jnp.clip(my_count - k, 0, 1).astype(jnp.float32)
        for t in range(ROWS // B):
            tile = phi_ref[k, pl.ds(t * B, B), :]
            tile = (tile.astype(jnp.float32) * live).T
            phit_ref[at, :, pl.ds(t * B, B)] = tile.astype(jnp.bfloat16)
        return carry

    lax.fori_loop(0, ENTRIES, turn, 0)
    rho_ref[...] = jnp.zeros_like(rho_ref)

    M, N = ENTRIES * GATHER_ROWS, 256
    one_round = stage_ref.at[pl.ds(0, (GROUPS - 1) * GATHER_ROWS)]

    def density_round(n, carry):
        pltpu.make_async_copy(one_round, one_round, drecv.at[n]).wait()
        rows = pl.ds(pl.multiple_of(n * GATHER_ROWS, GATHER_ROWS), GATHER_ROWS)

        def density(step, carry):
            cols = pl.ds(pl.multiple_of(step * N, N), N)
            g = jnp.dot(
                sub_ref[n], phit_ref[:, :, cols].reshape(WIDTH, N), preferred_element_type=jnp.float32
            )
            g = g * phit_ref[:, rows, cols].reshape(M, N).astype(jnp.float32)
            rho_ref[:, cols] += jnp.sum(g.reshape(M // 8, 8, N), axis=0)
            return carry

        return lax.fori_loop(0, ROWS // N, density, carry)

    lax.fori_loop(0, GATHER_ROUNDS, density_round, 0)

    rho = jnp.sum(rho_ref[...], axis=0, keepdims=True)
    pot_ref[...] = w_ref[...] * rho * jnp.exp(jnp.log(1.0 + rho * rho) * (-1.0 / 3.0))

    def weigh(c, carry):
        scaled_ref[c] = (
            phit_ref[pl.ds(c * 2, 2)].reshape(2 * B, ROWS).astype(jnp.float32) * pot_ref[...]
        ).astype(jnp.bfloat16)
        return carry

    lax.fori_loop(0, NCOL, weigh, 0)

    HALF = ENTRIES // 2

    def return_round(n, carry):
        rows = pl.ds(pl.multiple_of(n * RETURN_ROWS, RETURN_ROWS), RETURN_ROWS)

        def potential(step, carry):
            c, half = step // 2, step % 2
            v = lax.dot_general(
                phit_ref[pl.ds(half * HALF, HALF), rows, :].reshape(HALF * RETURN_ROWS, ROWS), scaled_ref[c],
                (((1,), (1,)), ((), ())), preferred_element_type=jnp.float32,
            ).astype(jnp.bfloat16).reshape(HALF, RETURN_ROWS, 2 * B)
            back_ref[n, c * 2, pl.ds(half * HALF, HALF)] = v[:, :, :B]
            back_ref[n, c * 2 + 1, pl.ds(half * HALF, HALF)] = v[:, :, B:]
            return carry

        lax.fori_loop(0, NCOL * 2, potential, 0)

        def main_copy(r, c):
            residue = (r + lag(r, c)) % NROW
            return pltpu.make_async_remote_copy(
                src_ref=back_ref.at[n, place(residue), place(r)],
                dst_ref=main_ref.at[n, me],
                send_sem=msend, recv_sem=mrecv,
                device_id=(r, c), device_id_type=MESH,
            )

        def far_copy(r, c):
            residue = (r + NCOL) % NROW
            return pltpu.make_async_remote_copy(
                src_ref=back_ref.at[n, place(residue), place(r)],
                dst_ref=far_ref.at[n, me],
                send_sem=fsend, recv_sem=frecv,
                device_id=(r, c), device_id_type=MESH,
            )

        def give(i, carry):
            r, c = offset_target(i, row, col)
            main_copy(r, c).start()

            @pl.when(lag(r, c) == 0)
            def _():
                far_copy(r, c).start()

            return carry

        lax.fori_loop(1, GROUPS, give, 0)
        residue = (row + lag(row, col)) % NROW
        own = pltpu.make_async_copy(back_ref.at[n, place(residue), place(row)], main_ref.at[n, me], self_sem)
        own.start()
        own.wait()

        @pl.when(lag(row, col) == 0)
        def _():
            residue = (row + NCOL) % NROW
            own = pltpu.make_async_copy(back_ref.at[n, place(residue), place(row)], far_ref.at[n, me], self_sem)
            own.start()
            own.wait()

        return carry

    lax.fori_loop(0, RETURN_ROUNDS, return_round, 0)

    every_block = stage_ref.at[pl.ds(0, (GROUPS - 1) * B // 2)]
    pltpu.make_async_copy(stage_ref.at[pl.ds(0, (GROUPS - 1) * B)], stage_ref.at[pl.ds(0, (GROUPS - 1) * B)], dsend).wait()
    pltpu.make_async_copy(every_block, every_block, msend).wait()
    pltpu.make_async_copy(every_block, every_block, mrecv).wait()

    @pl.when(lag(row, col) == 0)
    def _():
        others = stage_ref.at[pl.ds(0, (NROW - 1) * B // 2)]
        pltpu.make_async_copy(others, others, fsend).wait()
        pltpu.make_async_copy(every_block, every_block, frecv).wait()

    @pl.when(lag(row, col) != 0)
    def _():
        others = stage_ref.at[pl.ds(0, NROW * B // 2)]
        pltpu.make_async_copy(others, others, fsend).wait()


VMEM = pl.BlockSpec(memory_space=pltpu.VMEM)
SMEM = pl.BlockSpec(memory_space=pltpu.SMEM)
HBM = pl.BlockSpec(memory_space=pl.ANY)


def exchange(starts, cnt, w, dens, phi):
    parts = jax.ShapeDtypeStruct((RETURN_ROUNDS, GROUPS, RETURN_ROWS, B), jnp.bfloat16)
    return pl.pallas_call(
        group_kernel,
        out_shape=[parts, parts],
        in_specs=[SMEM, SMEM, VMEM, HBM, HBM],
        out_specs=[HBM, HBM],
        scratch_shapes=[
            pltpu.VMEM((ENTRIES, BLOCK_ROWS, B, B), jnp.bfloat16),
            pltpu.VMEM((ENTRIES, ROWS, B), jnp.bfloat16),
            pltpu.VMEM((NCOL, 2 * B, ROWS), jnp.bfloat16),
            pltpu.VMEM((ENTRIES, B, ROWS), jnp.bfloat16),
            pltpu.VMEM((GATHER_ROUNDS, ENTRIES * GATHER_ROWS, WIDTH), jnp.bfloat16),
            pltpu.VMEM((GROUPS * B, 2 * B), jnp.bfloat16),
            pltpu.VMEM((RETURN_ROUNDS, ENTRIES, ENTRIES, RETURN_ROWS, B), jnp.bfloat16),
            pltpu.VMEM((8, ROWS), jnp.float32),
            pltpu.VMEM((1, ROWS), jnp.float32),
            pltpu.SemaphoreType.DMA,
            pltpu.SemaphoreType.DMA,
            pltpu.SemaphoreType.DMA,
            pltpu.SemaphoreType.DMA((GATHER_ROUNDS,)),
            pltpu.SemaphoreType.DMA,
            pltpu.SemaphoreType.DMA,
            pltpu.SemaphoreType.DMA,
            pltpu.SemaphoreType.DMA,
            pltpu.SemaphoreType.DMA,
        ],
        compiler_params=pltpu.CompilerParams(
            collective_id=0, has_side_effects=True, vmem_limit_bytes=60 << 20
        ),
        cost_estimate=pl.CostEstimate(flops=4 * ROWS * WIDTH * WIDTH, bytes_accessed=32 << 20, transcendentals=2 * ROWS),
    )(starts, cnt, w, dens, phi)


CHUNK = 16


def sum_kernel(where_ref, start_ref, main_ref, far_ref, near_ref, wide_ref, turned_ref):
    row, col = where_ref[0], where_ref[1]
    n, step = pl.program_id(0), pl.program_id(1)
    shift = lag(row, col)
    rows = pl.ds(pl.multiple_of(n * RETURN_ROWS, RETURN_ROWS), RETURN_ROWS)

    @pl.when(step == 0)
    def _():
        near_ref[:, rows, :] = jnp.zeros((2 * BLOCK_ROWS, RETURN_ROWS, B), jnp.float32)
        wide_ref[:, rows, :] = jnp.zeros((2 * BLOCK_ROWS, RETURN_ROWS, B), jnp.float32)

    def slot(start, apart):
        k, l = list_place(start, row), list_place(start, row + apart)
        i = ((start + k) & (GROUPS - 1)) >> 4
        return i * 2 + (l < k).astype(jnp.int32)

    for m in range(CHUNK):
        at = slot(start_ref[step * CHUNK + m], shift)
        near_ref[at, rows, :] += main_ref[0, m].astype(jnp.float32)

    @pl.when(shift == 0)
    def _():
        for m in range(CHUNK):
            at = slot(start_ref[step * CHUNK + m], NCOL)
            wide_ref[at, rows, :] += far_ref[0, m].astype(jnp.float32)

    @pl.when((n == RETURN_ROUNDS - 1) & (step == GROUPS // CHUNK - 1))
    def _():
        for at in range(2 * BLOCK_ROWS):
            turned_ref[at] = near_ref[at].T.astype(jnp.bfloat16)


def collect(where, starts, main, far):
    def far_index(n, g, where_ref, start_ref):
        busy = (lag(where_ref[0], where_ref[1]) == 0).astype(jnp.int32)
        return n * busy, g * busy, 0, 0

    parts = (1, CHUNK, RETURN_ROWS, B)
    sums = (2 * BLOCK_ROWS, B, B)
    return pl.pallas_call(
        sum_kernel,
        grid_spec=pltpu.PrefetchScalarGridSpec(
            num_scalar_prefetch=2,
            grid=(RETURN_ROUNDS, GROUPS // CHUNK),
            in_specs=[
                pl.BlockSpec(parts, lambda n, g, where_ref, start_ref: (n, g, 0, 0)),
                pl.BlockSpec(parts, far_index),
            ],
            out_specs=[pl.BlockSpec(sums, lambda n, g, where_ref, start_ref: (0, 0, 0))] * 3,
        ),
        out_shape=[
            jax.ShapeDtypeStruct(sums, jnp.float32),
            jax.ShapeDtypeStruct(sums, jnp.float32),
            jax.ShapeDtypeStruct(sums, jnp.bfloat16),
        ],
        compiler_params=pltpu.CompilerParams(vmem_limit_bytes=40 << 20),
    )(where, starts, main, far)


SLOTS = 2 * BLOCK_ROWS


def relay_shift(i):
    return (5 * i + 1) % NROW, (3 * i) % NCOL


def mirror_owner(row, col):
    shift = lag(row, col)
    return (row + shift + NCOL * (shift == 0).astype(jnp.int32)) % NROW, row % NCOL


def mirror_source(row, col):
    return (row + lag(row, col) + NCOL) % NROW, row % NCOL


def mirror_kernel(turned_ref, out_ref, relay_ref, send1, recv1, send2, recv2):
    row, col = lax.axis_index("row"), lax.axis_index("col")
    me = row * NCOL + col

    def relay(i):
        dr, dc = relay_shift(i)
        return (row + dr) % NROW, (col + dc) % NCOL

    def origin(i):
        dr, dc = relay_shift(i)
        return (row - dr + NROW) % NROW, (col - dc + NCOL) % NCOL

    def final(i):
        return mirror_owner(*origin(i))

    barrier = pltpu.get_barrier_semaphore()
    source = mirror_source(row, col)
    expected = SLOTS
    for i in range(SLOTS):
        pl.semaphore_signal(barrier, inc=1, device_id=origin(i), device_id_type=MESH)
        dr, dc = relay_shift(i)
        r, c = (source[0] + dr) % NROW, (source[1] + dc) % NCOL

        @pl.when(r * NCOL + c != me)
        def _():
            pl.semaphore_signal(barrier, inc=1, device_id=(r, c), device_id_type=MESH)

        r, c = final(i)
        expected = expected + (r * NCOL + c != me).astype(jnp.int32)
    pl.semaphore_wait(barrier, expected)

    def first(i):
        return pltpu.make_async_remote_copy(
            src_ref=turned_ref.at[i], dst_ref=relay_ref.at[i], send_sem=send1.at[i], recv_sem=recv1.at[i],
            device_id=relay(i), device_id_type=MESH,
        )

    def second(i):
        return pltpu.make_async_remote_copy(
            src_ref=relay_ref.at[i], dst_ref=out_ref.at[i], send_sem=send2.at[i], recv_sem=recv2.at[i],
            device_id=final(i), device_id_type=MESH,
        )

    for i in range(SLOTS):
        first(i).start()
    for i in range(SLOTS):
        first(i).wait_recv()
        r, c = final(i)
        stays = r * NCOL + c == me

        @pl.when(jnp.logical_not(stays))
        def _():
            second(i).start()

        @pl.when(stays)
        def _():
            pltpu.make_async_copy(relay_ref.at[i], out_ref.at[i], recv2.at[i]).start()

    for i in range(SLOTS):
        first(i).wait_send()
        second(i).wait_recv()
        r, c = final(i)

        @pl.when(r * NCOL + c != me)
        def _():
            second(i).wait_send()


def mirror(turned):
    return pl.pallas_call(
        mirror_kernel,
        out_shape=jax.ShapeDtypeStruct((SLOTS, B, B), jnp.bfloat16),
        in_specs=[VMEM],
        out_specs=VMEM,
        scratch_shapes=[pltpu.VMEM((SLOTS, B, B), jnp.bfloat16)] + [pltpu.SemaphoreType.DMA((SLOTS,))] * 4,
        compiler_params=pltpu.CompilerParams(collective_id=1, has_side_effects=True),
    )(turned)


def place_kernel(where_ref, near_ref, wide_ref, mirrored_ref, out_ref):
    row, col = where_ref[0], where_ref[1]
    i = pl.program_id(0)
    shift = lag(row, col)
    out_ref[...] = jnp.zeros_like(out_ref)
    p = row + NROW * i

    def columns(q):
        return pl.ds(pl.multiple_of(((q & (GROUPS - 1)) >> 3) * B, B), B)

    @pl.when(shift == 0)
    def _():
        out_ref[:, columns(p)] = near_ref[i * 2]
        for w in range(2):
            out_ref[:, columns(p + NCOL - NROW * w)] = wide_ref[i * 2 + w]

    @pl.when(shift != 0)
    def _():
        for w in range(2):
            out_ref[:, columns(p + shift - NROW * w)] = near_ref[i * 2 + w]
            there = p - (NCOL - shift) + NROW * w
            at = ((there & (GROUPS - 1)) >> 4) * 2 + w
            out_ref[:, columns(there)] = mirrored_ref[at].astype(jnp.float32)


def assemble(where, near, wide, mirrored):
    return pl.pallas_call(
        place_kernel,
        grid=(BLOCK_ROWS,),
        out_shape=jax.ShapeDtypeStruct((BLOCK_ROWS * B, WIDTH), jnp.float32),
        in_specs=[SMEM, VMEM, VMEM, VMEM],
        out_specs=pl.BlockSpec((B, WIDTH), lambda i: (i, 0)),
    )(where, near, wide, mirrored)


def body(basis_values, point_weights, density_stored, relevant_blocks, relevant_count, block_home):
    starts = block_home[relevant_blocks[:, 0]]
    main, far = exchange(
        starts, relevant_count, point_weights.reshape(1, ROWS),
        density_stored.reshape(BLOCK_ROWS, B, WIDTH), basis_values,
    )
    where = jnp.stack([lax.axis_index("row"), lax.axis_index("col")]).astype(jnp.int32)
    near, wide, turned = collect(where, starts, main, far)
    return assemble(where, near, wide, mirror(turned))


def solution(mesh):
    in_specs = (P(("row", "col"), None), P(("row", "col")), P("row", "col"), P(), P(), P())
    return jax.shard_map(body, mesh=mesh, in_specs=in_specs, out_specs=P("row", "col"), check_vma=False)
```

time: 297 us -> 249 us (0.84)
  the two profiles are of different devices: /device:TPU:23 before, /device:TPU:0 now
where the time goes in v2:
time: 249 us
  Pallas kernels  238 us (96%)
  local copies, waits for them, and re-layouts  10.2 us (4%)
    pallas_call x1, Pallas kernels, exchange(): pl.pallas_call(group_kernel, out_shape=[parts, parts], in_specs=[SMEM, SM...  202 us
    pallas_call x1, Pallas kernels, mirror(): pl.pallas_call(mirror_kernel, out_shape=jax.ShapeDtypeStruct((SLOTS, B, B...  24.4 us
    unnamed x16, local copies, waits for them, and re-layouts  7.15 us
    pallas_call x1, Pallas kernels, assemble(): pl.pallas_call(place_kernel, grid=(BLOCK_ROWS,), out_shape=jax.ShapeDtype...  6.31 us

profile of v2, /device:TPU:0, one launch (start us, length us, event | category | flops | bytes accessed | tf_op | source)
XLA Modules:
  0.0 248.6 jit_solution(9344987489969212110)
XLA Ops:
  0.0 0.0 copy-start
  0.0 0.1 pad_add_fusion.where_ref
  0.1 0.0 copy-start.6
  0.1 0.7 fusion
  0.8 0.0 copy-done
  0.8 1.8 gather_fusion
  2.6 1.3 reshape.6.w_ref
  3.9 0.0 copy-start.7
  3.9 202.1 %shard_map.64 = (bf16[2,128,64,128]{3,2,1,0:T(8,128)(2,1)}, bf16[2,128,64,128]{3,2,1,0:T(8,128)(2,1)}) custom-call(s32[128]{0:T(128)} %gather_fusion, s32[128]{0:T(128)} %cnt_ref.1, f32[1,1536]{1,0:T(1,128)} %reshape.6.w_ref, bf16[8,128,2048]{2,1,0:T(8,128)(2,1)} %bitcast.5, bf16[1536,2048]{1,0:T(8,128)(2,1)} %phi_hbm.1), custom_call_target="tpu_custom_call" | custom-call | flops 25769803776 | bytes 33554432 | tf_op jit(solution)/shard_map/pallas_call | solution.py:253
  205.9 0.0 copy-done.6
  205.9 0.0 copy-done.7
  205.9 0.0 copy-start.1
  206.0 2.2 copy-done.1
  208.1 0.0 copy-start.2
  208.1 2.2 copy-done.2
  210.3 4.8 %shard_map.65 = (f32[16,128,128]{2,1,0:T(8,128)S(1)}, f32[16,128,128]{2,1,0:T(8,128)S(1)}, bf16[16,128,128]{2,1,0:T(8,128)(2,1)S(1)}) custom-call(s32[2]{0:T(128)S(1)} %pad_add_fusion.where_ref, s32[128]{0:T(128)S(1)} %copy-done.7, bf16[2,128,64,128]{3,2,1,0:T(8,128)(2,1)S(1)} %copy-done.1, bf16[2,128,64,128]{3,2,1,0:T(8,128)(2,1)S(1)} %copy-done.2), custom_call_target="tpu_custom_call" | custom-call | tf_op jit(solution)/shard_map/pallas_call | solution.py:327
  215.1 0.0 copy-start.3
  215.1 1.0 copy-done.3
  216.1 0.0 copy-start.4
  216.1 1.0 copy-done.4
  217.1 0.0 copy-start.5
  217.1 0.8 copy-done.5
  217.9 24.4 %shard_map.66.mirrored_ref = bf16[16,128,128]{2,1,0:T(8,128)(2,1)} custom-call(bf16[16,128,128]{2,1,0:T(8,128)(2,1)} %copy-done.5), custom_call_target="tpu_custom_call" | custom-call | tf_op jit(solution)/shard_map/pallas_call | solution.py:432
  242.3 6.3 %shard_map.67 = f32[1024,2048]{1,0:T(8,128)} custom-call(s32[2]{0:T(128)} %copy-done.6, f32[16,128,128]{2,1,0:T(8,128)} %copy-done.3, f32[16,128,128]{2,1,0:T(8,128)} %copy-done.4, bf16[16,128,128]{2,1,0:T(8,128)(2,1)} %shard_map.66.mirrored_ref), custom_call_target="tpu_custom_call" | custom-call | tf_op jit(solution)/shard_map/pallas_call | solution.py:468
  (1 shorter events, 0.0 us)
Async XLA Ops:
  0.0 0.8 copy-start
  0.1 205.9 %copy-start.6 = (s32[2]{0:T(128)}, s32[2]{0:T(128)S(1)}, u32[]{:S(2)}) copy-start(s32[2]{0:T(128)S(1)} %pad_add_fusion.where_ref) | copy-start | bytes 28
  3.9 202.1 %copy-start.7 = (s32[128]{0:T(128)S(1)}, s32[128]{0:T(128)}, u32[]{:S(2)}) copy-start(s32[128]{0:T(128)} %gather_fusion) | copy-start | bytes 1540
  205.9 2.2 copy-start.1
  208.1 2.2 copy-start.2
  215.1 1.0 copy-start.3
  216.1 1.0 copy-start.4
  217.1 0.8 copy-start.5

commit v3 on v2

v3 whole, which is shorter than its diff:
```python
import jax
import jax.numpy as jnp
from jax import lax
from jax.experimental import pallas as pl
from jax.experimental.pallas import tpu as pltpu
from jax.sharding import PartitionSpec as P

MESH = pl.DeviceIdType.MESH
NROW, NCOL, GROUPS, B = 16, 8, 128, 128
ENTRIES = 16
ROWS = 1536
WIDTH = ENTRIES * B
BLOCK_ROWS = 8
GATHER_ROUNDS, GATHER_ROWS = 4, 32
RETURN_ROUNDS, RETURN_ROWS = 2, 64
RUN = 32
SLOTS = 2 * BLOCK_ROWS


def place(residue):
    return (residue % NCOL) * 2 + residue // NCOL


def offset_target(step, row, col):
    t = (step * (step + 1) // 2) % GROUPS
    y = (row // 4 + t % 4) % 4
    x = (row % 4 + (t // 4) % 4) % 4
    z = (col // 2 + (t // 16) % 4) % 4
    core = (col + t // 64) % 2
    return y * 4 + x, z * 2 + core


def list_place(start, residue):
    return (residue - start) & (ENTRIES - 1)


def position(start, residue):
    return (start + list_place(start, residue)) & (GROUPS - 1)


def lag(row, col):
    return (col - row + NROW) % NCOL


def mirror_owner(row, col):
    shift = lag(row, col)
    return (row + shift + NCOL * (shift == 0).astype(jnp.int32)) % NROW, row % NCOL


def group_kernel(
    start_ref, order_ref, below_ref, cnt_ref, w_ref, dens_hbm, phi_hbm, near_ref, wide_ref, mirrored_ref,
    dens_ref, phi_ref, scaled_ref, phit_ref, sub_ref, stage_ref, back_ref, rho_ref, pot_ref,
    main0_ref, main1_ref, far0_ref, far1_ref, run_ref, turned_ref, relay_ref, keep_ref,
    dens_sem, phi_sem, dsend, drecv, msend, mrecv, fsend, frecv, self_sem, send1, recv1, send2, recv2,
):
    row, col = lax.axis_index("row"), lax.axis_index("col")
    me = row * NCOL + col

    def column(k):
        return pl.ds(k * B, B)

    dens_copies = [
        pltpu.make_async_copy(dens_hbm.at[:, :, column(k)], dens_ref.at[k], dens_sem) for k in range(ENTRIES)
    ]
    for copy in dens_copies:
        copy.start()

    def load_phi(half):
        for k in range(ENTRIES):
            pltpu.make_async_copy(
                phi_hbm.at[pl.ds(half * (ROWS // 2), ROWS // 2), column(k)], phi_ref.at[k], phi_sem
            ).start()

    load_phi(0)

    barrier = pltpu.get_barrier_semaphore()

    def greet(i, carry):
        r, c = offset_target(i, row, col)
        pl.semaphore_signal(barrier, inc=1, device_id=(r, c), device_id_type=MESH)
        return carry

    lax.fori_loop(1, GROUPS, greet, 0)

    def pick(r, c):
        start = start_ref[r * NCOL + c]
        i = position(start, row) >> 4
        j0 = position(start, col) >> 3
        j1 = position(start, col + NCOL) >> 3
        return dens_ref[j0, i], dens_ref[j1, i]

    pltpu.make_async_copy(dens_ref, dens_ref, dens_sem).wait()

    def staged(n, r, c):
        at = (n * GROUPS + r * NCOL + c) * GATHER_ROWS
        return pl.ds(pl.multiple_of(at, GATHER_ROWS), GATHER_ROWS)

    def prepare(i, carry):
        r, c = offset_target(i, row, col)
        left, right = pick(r, c)
        for n in range(GATHER_ROUNDS):
            part = slice(n * GATHER_ROWS, (n + 1) * GATHER_ROWS)
            stage_ref[staged(n, r, c), pl.ds(0, B)] = left[part]
            stage_ref[staged(n, r, c), pl.ds(B, B)] = right[part]
        return carry

    lax.fori_loop(1, GROUPS, prepare, 0)
    my_rows = pl.ds(pl.multiple_of(place(row) * GATHER_ROWS, GATHER_ROWS), GATHER_ROWS)
    my_cols = pl.ds(pl.multiple_of(col * 2 * B, B), 2 * B)
    left, right = pick(row, col)
    for n in range(GATHER_ROUNDS):
        part = slice(n * GATHER_ROWS, (n + 1) * GATHER_ROWS)
        sub_ref[n, my_rows, my_cols] = jnp.concatenate([left[part], right[part]], axis=1)

    pl.semaphore_wait(barrier, GROUPS - 1)

    def send_round(n, carry):
        def send(i, carry):
            r, c = offset_target(i, row, col)
            pltpu.make_async_remote_copy(
                src_ref=stage_ref.at[staged(n, r, c)],
                dst_ref=sub_ref.at[n, my_rows, my_cols],
                send_sem=dsend, recv_sem=drecv.at[n],
                device_id=(r, c), device_id_type=MESH,
            ).start()
            return carry

        return lax.fori_loop(1, GROUPS, send, carry)

    lax.fori_loop(0, GATHER_ROUNDS, send_round, 0)

    my_start = start_ref[me]
    my_count = cnt_ref[me]

    for half in range(2):
        pltpu.make_async_copy(phi_ref, phi_ref, phi_sem).wait()

        def turn(at, carry):
            residue = at // 2 + (at % 2) * NCOL
            k = list_place(my_start, residue)
            live = jnp.clip(my_count - k, 0, 1).astype(jnp.float32)
            for t in range(ROWS // 2 // B):
                tile = phi_ref[k, pl.ds(t * B, B), :]
                tile = (tile.astype(jnp.float32) * live).T
                phit_ref[at, :, pl.ds(half * (ROWS // 2) + t * B, B)] = tile.astype(jnp.bfloat16)
            return carry

        lax.fori_loop(0, ENTRIES, turn, 0)
        if half == 0:
            load_phi(1)

    shift = lag(row, col)

    def segment(start, apart):
        k = list_place(start, row)
        whole = jnp.clip(ENTRIES - apart - k, 0, 1)
        return ((start + k) >> 4) * 2 + whole

    def keeps(m, carry):
        for at, apart in ((0, shift), (1, NCOL)):
            same = 1 - jnp.clip(segment(start_ref[order_ref[m]], apart) - segment(start_ref[order_ref[m - 1]], apart), 0, 1)
            keep_ref[at, m] = same.astype(jnp.float32)
        return carry

    keep_ref[0, 0] = 0.0
    keep_ref[1, 0] = 0.0
    lax.fori_loop(1, GROUPS, keeps, 0)
    rho_ref[...] = jnp.zeros_like(rho_ref)

    M, N = ENTRIES * GATHER_ROWS, 256
    one_round = stage_ref.at[pl.ds(0, (GROUPS - 1) * GATHER_ROWS)]

    def density_round(n, carry):
        pltpu.make_async_copy(one_round, one_round, drecv.at[n]).wait()
        rows = pl.ds(pl.multiple_of(n * GATHER_ROWS, GATHER_ROWS), GATHER_ROWS)

        def density(step, carry):
            cols = pl.ds(pl.multiple_of(step * N, N), N)
            g = jnp.dot(
                sub_ref[n], phit_ref[:, :, cols].reshape(WIDTH, N), preferred_element_type=jnp.float32
            )
            g = g * phit_ref[:, rows, cols].reshape(M, N).astype(jnp.float32)
            rho_ref[:, cols] += jnp.sum(g.reshape(M // 8, 8, N), axis=0)
            return carry

        return lax.fori_loop(0, ROWS // N, density, carry)

    lax.fori_loop(0, GATHER_ROUNDS, density_round, 0)

    rho = jnp.sum(rho_ref[...], axis=0, keepdims=True)
    pot_ref[...] = w_ref[...] * rho * jnp.exp(jnp.log(1.0 + rho * rho) * (-1.0 / 3.0))

    def weigh(c, carry):
        scaled_ref[c] = (
            phit_ref[pl.ds(c * 2, 2)].reshape(2 * B, ROWS).astype(jnp.float32) * pot_ref[...]
        ).astype(jnp.bfloat16)
        return carry

    lax.fori_loop(0, NCOL, weigh, 0)

    HALF = ENTRIES // 2
    main_refs, far_refs = (main0_ref, main1_ref), (far0_ref, far1_ref)

    def return_round(n):
        rows = pl.ds(pl.multiple_of(n * RETURN_ROWS, RETURN_ROWS), RETURN_ROWS)

        def potential(step, carry):
            c, half = step // 2, step % 2
            v = lax.dot_general(
                phit_ref[pl.ds(half * HALF, HALF), rows, :].reshape(HALF * RETURN_ROWS, ROWS), scaled_ref[c],
                (((1,), (1,)), ((), ())), preferred_element_type=jnp.float32,
            ).astype(jnp.bfloat16).reshape(HALF, RETURN_ROWS, 2 * B)
            back_ref[n, c * 2, pl.ds(half * HALF, HALF)] = v[:, :, :B]
            back_ref[n, c * 2 + 1, pl.ds(half * HALF, HALF)] = v[:, :, B:]
            return carry

        lax.fori_loop(0, NCOL * 2, potential, 0)

        def main_copy(r, c):
            residue = (r + lag(r, c)) % NROW
            return pltpu.make_async_remote_copy(
                src_ref=back_ref.at[n, place(residue), place(r)],
                dst_ref=main_refs[n].at[me],
                send_sem=msend, recv_sem=mrecv.at[n],
                device_id=(r, c), device_id_type=MESH,
            )

        def far_copy(r, c):
            residue = (r + NCOL) % NROW
            return pltpu.make_async_remote_copy(
                src_ref=back_ref.at[n, place(residue), place(r)],
                dst_ref=far_refs[n].at[me],
                send_sem=fsend, recv_sem=frecv.at[n],
                device_id=(r, c), device_id_type=MESH,
            )

        def give(i, carry):
            r, c = offset_target(i, row, col)
            main_copy(r, c).start()

            @pl.when(lag(r, c) == 0)
            def _():
                far_copy(r, c).start()

            return carry

        lax.fori_loop(1, GROUPS, give, 0)
        residue = (row + lag(row, col)) % NROW
        own = pltpu.make_async_copy(back_ref.at[n, place(residue), place(row)], main_refs[n].at[me], self_sem)
        own.start()
        own.wait()

        @pl.when(lag(row, col) == 0)
        def _():
            residue = (row + NCOL) % NROW
            own = pltpu.make_async_copy(back_ref.at[n, place(residue), place(row)], far_refs[n].at[me], self_sem)
            own.start()
            own.wait()

    for n in range(RETURN_ROUNDS):
        return_round(n)
    gathered = stage_ref.at[pl.ds(0, (GROUPS - 1) * B)]
    pltpu.make_async_copy(gathered, gathered, dsend).wait()

    def relay_shift(i):
        return (5 * i + 1) % NROW, (3 * i) % NCOL

    def relay(i):
        dr, dc = relay_shift(i)
        return (row + dr) % NROW, (col + dc) % NCOL

    def final(i):
        dr, dc = relay_shift(i)
        return mirror_owner((row - dr + NROW) % NROW, (col - dc + NCOL) % NCOL)

    def first(n, i):
        return pltpu.make_async_remote_copy(
            src_ref=turned_ref.at[n, i], dst_ref=relay_ref.at[n, i], send_sem=send1.at[n, i], recv_sem=recv1.at[n, i],
            device_id=relay(i), device_id_type=MESH,
        )

    def second(n, i):
        return pltpu.make_async_remote_copy(
            src_ref=relay_ref.at[n, i], dst_ref=mirrored_ref.at[n, i], send_sem=send2.at[n, i], recv_sem=recv2.at[n, i],
            device_id=final(i), device_id_type=MESH,
        )

    def stays(i):
        r, c = final(i)
        return r * NCOL + c == me

    def total(parts_ref, n, which, apart, out_ref):
        for u in range(RETURN_ROWS // RUN):
            rows = pl.ds(u * RUN, RUN)

            def add(m, acc):
                acc = acc * keep_ref[which, m] + parts_ref[order_ref[m], rows, :].astype(jnp.float32)
                run_ref[m] = acc
                return acc

            lax.fori_loop(0, GROUPS, add, jnp.zeros((RUN, B), jnp.float32))
            out_rows = pl.ds(pl.multiple_of(n * RETURN_ROWS + u * RUN, RUN), RUN)

            def slot(at, carry):
                i, w = at // 2, at % 2

                def ended(i):
                    p = row + i * NROW
                    low = jnp.where(w == 1, p - 15, p - 15 + apart)
                    high = jnp.where(w == 1, p - 15 + apart, p + 1)
                    before = below_ref[jnp.clip(low, 0, GROUPS)]
                    until = below_ref[jnp.clip(high, 0, GROUPS)]
                    some = jnp.clip(until - before, 0, 1).astype(jnp.float32)
                    return run_ref[jnp.maximum(until - 1, 0)] * some

                out_ref[at, out_rows, :] = ended(i)

                @pl.when(i == 0)
                def _():
                    out_ref[at, out_rows, :] += ended(BLOCK_ROWS)

                return carry

            lax.fori_loop(0, SLOTS, slot, 0)

    one_part = stage_ref.at[pl.ds(0, (GROUPS - 1) * RETURN_ROWS // 2)]

    def finish_round(n):
        pltpu.make_async_copy(one_part, one_part, mrecv.at[n]).wait()
        total(main_refs[n], n, 0, shift, near_ref)

        def start_first(i, carry):
            rows = pl.ds(pl.multiple_of(n * RETURN_ROWS, RETURN_ROWS), RETURN_ROWS)
            turned_ref[n, i] = near_ref[i, rows, :].astype(jnp.bfloat16)
            first(n, i).start()
            return carry

        lax.fori_loop(0, SLOTS, start_first, 0)

        @pl.when(shift == 0)
        def _():
            pltpu.make_async_copy(one_part, one_part, frecv.at[n]).wait()
            total(far_refs[n], n, 1, NCOL, wide_ref)

        def pass_on(i, carry):
            first(n, i).wait_recv()

            @pl.when(jnp.logical_not(stays(i)))
            def _():
                second(n, i).start()

            @pl.when(stays(i))
            def _():
                pltpu.make_async_copy(relay_ref.at[n, i], mirrored_ref.at[n, i], recv2.at[n, i]).start()

            return carry

        lax.fori_loop(0, SLOTS, pass_on, 0)

    @pl.when(shift != 0)
    def _():
        wide_ref[...] = jnp.zeros_like(wide_ref)

    for n in range(RETURN_ROUNDS):
        finish_round(n)

    def done(at, carry):
        n, i = at // SLOTS, at % SLOTS
        first(n, i).wait_send()
        second(n, i).wait_recv()

        @pl.when(jnp.logical_not(stays(i)))
        def _():
            second(n, i).wait_send()

        return carry

    lax.fori_loop(0, RETURN_ROUNDS * SLOTS, done, 0)

    sent = stage_ref.at[pl.ds(0, (GROUPS - 1) * B // 2)]
    pltpu.make_async_copy(sent, sent, msend).wait()

    @pl.when(shift == 0)
    def _():
        others = stage_ref.at[pl.ds(0, (NROW - 1) * B // 2)]
        pltpu.make_async_copy(others, others, fsend).wait()

    @pl.when(shift != 0)
    def _():
        others = stage_ref.at[pl.ds(0, NROW * B // 2)]
        pltpu.make_async_copy(others, others, fsend).wait()


VMEM = pl.BlockSpec(memory_space=pltpu.VMEM)
SMEM = pl.BlockSpec(memory_space=pltpu.SMEM)
HBM = pl.BlockSpec(memory_space=pl.ANY)


def exchange(starts, order, below, cnt, w, dens, phi):
    sums = jax.ShapeDtypeStruct((SLOTS, B, B), jnp.float32)
    parts = (GROUPS, RETURN_ROWS, B)
    slots = (RETURN_ROUNDS, SLOTS, RETURN_ROWS, B)
    dma = pltpu.SemaphoreType.DMA
    return pl.pallas_call(
        group_kernel,
        out_shape=[sums, sums, jax.ShapeDtypeStruct(slots, jnp.bfloat16)],
        in_specs=[SMEM, SMEM, SMEM, SMEM, VMEM, HBM, HBM],
        out_specs=[VMEM, VMEM, VMEM],
        scratch_shapes=[
            pltpu.VMEM((ENTRIES, BLOCK_ROWS, B, B), jnp.bfloat16),
            pltpu.VMEM((ENTRIES, ROWS // 2, B), jnp.bfloat16),
            pltpu.VMEM((NCOL, 2 * B, ROWS), jnp.bfloat16),
            pltpu.VMEM((ENTRIES, B, ROWS), jnp.bfloat16),
            pltpu.VMEM((GATHER_ROUNDS, ENTRIES * GATHER_ROWS, WIDTH), jnp.bfloat16),
            pltpu.VMEM((GROUPS * B, 2 * B), jnp.bfloat16),
            pltpu.VMEM((RETURN_ROUNDS, ENTRIES, ENTRIES, RETURN_ROWS, B), jnp.bfloat16),
            pltpu.VMEM((8, ROWS), jnp.float32),
            pltpu.VMEM((1, ROWS), jnp.float32),
            pltpu.VMEM(parts, jnp.bfloat16),
            pltpu.VMEM(parts, jnp.bfloat16),
            pltpu.VMEM(parts, jnp.bfloat16),
            pltpu.VMEM(parts, jnp.bfloat16),
            pltpu.VMEM((GROUPS, RUN, B), jnp.float32),
            pltpu.VMEM(slots, jnp.bfloat16),
            pltpu.VMEM(slots, jnp.bfloat16),
            pltpu.SMEM((2, GROUPS), jnp.float32),
            dma, dma, dma, dma((GATHER_ROUNDS,)), dma, dma((RETURN_ROUNDS,)), dma, dma((RETURN_ROUNDS,)), dma,
        ] + [dma((RETURN_ROUNDS, SLOTS))] * 4,
        compiler_params=pltpu.CompilerParams(
            collective_id=0, has_side_effects=True, vmem_limit_bytes=61 << 20
        ),
        cost_estimate=pl.CostEstimate(flops=4 * ROWS * WIDTH * WIDTH, bytes_accessed=16 << 20, transcendentals=2 * ROWS),
    )(starts, order, below, cnt, w, dens, phi)


def sort_kernel(list_ref, home_ref, start_ref, order_ref, below_ref, next_ref):
    def clear(v, carry):
        below_ref[v] = 0
        return carry

    def count(g, carry):
        start = home_ref[list_ref[g, 0]]
        start_ref[g] = start
        below_ref[start + 1] += 1
        return carry

    def add(v, before):
        before = before + below_ref[v]
        below_ref[v] = before
        next_ref[v] = before
        return before

    def put(g, carry):
        start = start_ref[g]
        at = next_ref[start]
        order_ref[at] = g
        next_ref[start] = at + 1
        return carry

    lax.fori_loop(0, GROUPS + 8, clear, 0, unroll=8)
    lax.fori_loop(0, GROUPS, count, 0, unroll=8)
    lax.fori_loop(0, GROUPS + 8, add, 0, unroll=8)
    lax.fori_loop(0, GROUPS, put, 0, unroll=8)


def sort_starts(lists, home):
    return pl.pallas_call(
        sort_kernel,
        out_shape=[
            jax.ShapeDtypeStruct((GROUPS,), jnp.int32),
            jax.ShapeDtypeStruct((GROUPS,), jnp.int32),
            jax.ShapeDtypeStruct((GROUPS + 8,), jnp.int32),
        ],
        in_specs=[SMEM, SMEM],
        out_specs=[SMEM, SMEM, SMEM],
        scratch_shapes=[pltpu.SMEM((GROUPS + 8,), jnp.int32)],
    )(lists, home)


def place_kernel(where_ref, near_ref, wide_ref, mirrored_ref, out_ref):
    row, col = where_ref[0], where_ref[1]
    i = pl.program_id(0)
    shift = lag(row, col)
    out_ref[...] = jnp.zeros_like(out_ref)
    p = row + NROW * i

    def columns(q):
        return pl.ds(pl.multiple_of(((q & (GROUPS - 1)) >> 3) * B, B), B)

    @pl.when(shift == 0)
    def _():
        out_ref[:, columns(p)] = near_ref[i * 2]
        for w in range(2):
            out_ref[:, columns(p + NCOL - NROW * w)] = wide_ref[i * 2 + w]

    @pl.when(shift != 0)
    def _():
        for w in range(2):
            out_ref[:, columns(p + shift - NROW * w)] = near_ref[i * 2 + w]
            there = p - (NCOL - shift) + NROW * w
            at = ((there & (GROUPS - 1)) >> 4) * 2 + w
            block = jnp.concatenate([mirrored_ref[n, at] for n in range(RETURN_ROUNDS)], axis=0)
            out_ref[:, columns(there)] = block.astype(jnp.float32).T


def assemble(where, near, wide, mirrored):
    return pl.pallas_call(
        place_kernel,
        grid=(BLOCK_ROWS,),
        out_shape=jax.ShapeDtypeStruct((BLOCK_ROWS * B, WIDTH), jnp.float32),
        in_specs=[SMEM, VMEM, VMEM, VMEM],
        out_specs=pl.BlockSpec((B, WIDTH), lambda i: (i, 0)),
    )(where, near, wide, mirrored)


def body(basis_values, point_weights, density_stored, relevant_blocks, relevant_count, block_home):
    starts, order, below = sort_starts(relevant_blocks, block_home)
    near, wide, mirrored = exchange(
        starts, order, below, relevant_count, point_weights.reshape(1, ROWS),
        density_stored.reshape(BLOCK_ROWS, B, WIDTH), basis_values,
    )
    where = jnp.stack([lax.axis_index("row"), lax.axis_index("col")]).astype(jnp.int32)
    return assemble(where, near, wide, mirrored)


def solution(mesh):
    in_specs = (P(("row", "col"), None), P(("row", "col")), P("row", "col"), P(), P(), P())
    return jax.shard_map(body, mesh=mesh, in_specs=in_specs, out_specs=P("row", "col"), check_vma=False)
```

time: 249 us -> 246 us (0.988)
  local copies, waits for them, and re-layouts: 10.2 us -> 2.72 us
  Pallas kernels: 238 us -> 242 us
    unnamed x16 -> x1, local copies, waits for them, and re-layouts: 7.15 us -> 1.42 us
    pallas_call x3 -> x2, Pallas kernels: 231 us -> 236 us  [the longest x1 231 us: exchange(): pl.pallas_call(group_kernel, out_shape=[sums, sums, jax.ShapeDtypeStruct(...]
where the time goes in v3:
time: 246 us; the launch traced here: 245 us
  Pallas kernels  242 us (98%)
  local copies, waits for them, and re-layouts  2.72 us (1%)
    pallas_call x1, Pallas kernels, exchange(): pl.pallas_call(group_kernel, out_shape=[sums, sums, jax.ShapeDtypeStruct(...  231 us
    pallas_call x1, Pallas kernels, assemble(): pl.pallas_call(place_kernel, grid=(BLOCK_ROWS,), out_shape=jax.ShapeDtype...  6.31 us

profile of v3, /device:TPU:0, one launch (start us, length us, event | category | flops | bytes accessed | tf_op | source)
XLA Modules:
  0.0 245.3 jit_solution(2540172018829122146)
XLA Ops:
  0.0 0.7 pad_add_fusion.where_ref
  0.7 1.3 reshape.6.w_ref
  2.0 1.4 copy.7.list_ref
  3.4 4.4 %shard_map.64 = (s32[128]{0:T(128)}, s32[128]{0:T(128)}, s32[136]{0:T(256)}) custom-call(s32[128,16]{1,0:T(8,128)} %copy.7.list_ref, s32[128]{0:T(128)} %home_ref.1), custom_call_target="tpu_custom_call" | custom-call | tf_op jit(solution)/shard_map/pallas_call | solution.py:467
  7.8 231.2 %shard_map.65 = (f32[16,128,128]{2,1,0:T(8,128)}, f32[16,128,128]{2,1,0:T(8,128)}, bf16[2,16,64,128]{3,2,1,0:T(8,128)(2,1)}) custom-call(s32[128]{0:T(128)} %get-tuple-element.11.start_ref, s32[128]{0:T(128)} %get-tuple-element.12.order_ref, s32[136]{0:T(256)} %get-tuple-element.13.below_ref, s32[128]{0:T(128)} %cnt_ref.1, f32[1,1536]{1,0:T(1,128)} %reshape.6.w_ref, ...), custom_call_target="tpu_custom_call" | custom-call | flops 25769803776 | bytes 16777216 | tf_op jit(solution)/shard_map/pallas_call | solution.py:404
  239.0 6.3 %shard_map.66 = f32[1024,2048]{1,0:T(8,128)} custom-call(s32[2]{0:T(128)} %pad_add_fusion.where_ref, f32[16,128,128]{2,1,0:T(8,128)} %get-tuple-element.14.near_ref, f32[16,128,128]{2,1,0:T(8,128)} %get-tuple-element.15.wide_ref, bf16[2,16,64,128]{3,2,1,0:T(8,128)(2,1)} %get-tuple-element.16.mirrored_ref), custom_call_target="tpu_custom_call" | custom-call | tf_op jit(solution)/shard_map/pallas_call | solution.py:507

commit v4 on v3

--- a/solution.py
+++ b/solution.py
@@ -48,13 +48,16 @@
 
 
 def group_kernel(
-    start_ref, order_ref, below_ref, cnt_ref, w_ref, dens_hbm, phi_hbm, near_ref, wide_ref, mirrored_ref,
+    first_ref, home_ref, first_row, home_row, cnt_ref, w_ref, dens_hbm, phi_hbm, near_ref, wide_ref, mirrored_ref,
     dens_ref, phi_ref, scaled_ref, phit_ref, sub_ref, stage_ref, back_ref, rho_ref, pot_ref,
-    main0_ref, main1_ref, far0_ref, far1_ref, run_ref, turned_ref, relay_ref, keep_ref,
-    dens_sem, phi_sem, dsend, drecv, msend, mrecv, fsend, frecv, self_sem, send1, recv1, send2, recv2,
+    main_refs, far_refs, run_ref, turned_ref, relay_ref, keep_ref, table_ref, order_ref,
+    table_sem, dens_sem, phi_sem, dsend, drecv, msend, mrecv, fsend, frecv, self_sem, send1, recv1, send2, recv2,
 ):
     row, col = lax.axis_index("row"), lax.axis_index("col")
     me = row * NCOL + col
+
+    def start_of(group):
+        return home_ref[first_ref[0, group]]
 
     def column(k):
         return pl.ds(k * B, B)
@@ -83,7 +86,7 @@
     lax.fori_loop(1, GROUPS, greet, 0)
 
     def pick(r, c):
-        start = start_ref[r * NCOL + c]
+        start = start_of(r * NCOL + c)
         i = position(start, row) >> 4
         j0 = position(start, col) >> 3
         j1 = position(start, col + NCOL) >> 3
@@ -129,7 +132,7 @@
 
     lax.fori_loop(0, GATHER_ROUNDS, send_round, 0)
 
-    my_start = start_ref[me]
+    my_start = start_of(me)
     my_count = cnt_ref[me]
 
     for half in range(2):
@@ -151,6 +154,25 @@
 
     shift = lag(row, col)
 
+    lane = lax.broadcasted_iota(jnp.int32, (GROUPS, GROUPS), 1)
+    line = lax.broadcasted_iota(jnp.int32, (GROUPS, GROUPS), 0)
+    homes = jnp.broadcast_to(home_row[...], (GROUPS, GROUPS)).T
+    starts = jnp.sum(jnp.where(first_row[0:1, :] == line, homes, 0), axis=0, keepdims=True)
+    across = jnp.broadcast_to(starts, (GROUPS, GROUPS))
+    down = across.T
+    ahead = ((across < down) | ((across == down) & (lane < line))).astype(jnp.int32)
+    rank = jnp.sum(ahead, axis=1, keepdims=True)
+    table_ref[0:1, :] = jnp.sum(jnp.where(rank == lane, line, 0), axis=0, keepdims=True)
+    table_ref[1:2, :] = jnp.sum((down < lane).astype(jnp.int32), axis=0, keepdims=True)
+    table_ref[2:3, :] = jnp.sum((down < lane + GROUPS).astype(jnp.int32), axis=0, keepdims=True)
+    table_ref[3:4, :] = jnp.sum(jnp.where(rank == lane, down, 0), axis=0, keepdims=True)
+    tables = pltpu.make_async_copy(table_ref, order_ref, table_sem)
+    tables.start()
+    tables.wait()
+
+    def below(at):
+        return order_ref[1 + at // GROUPS, at % GROUPS]
+
     def segment(start, apart):
         k = list_place(start, row)
         whole = jnp.clip(ENTRIES - apart - k, 0, 1)
@@ -158,7 +180,7 @@
 
     def keeps(m, carry):
         for at, apart in ((0, shift), (1, NCOL)):
-            same = 1 - jnp.clip(segment(start_ref[order_ref[m]], apart) - segment(start_ref[order_ref[m - 1]], apart), 0, 1)
+            same = 1 - jnp.clip(segment(order_ref[3, m], apart) - segment(order_ref[3, m - 1], apart), 0, 1)
             keep_ref[at, m] = same.astype(jnp.float32)
         return carry
 
@@ -188,7 +210,7 @@
     lax.fori_loop(0, GATHER_ROUNDS, density_round, 0)
 
     rho = jnp.sum(rho_ref[...], axis=0, keepdims=True)
-    pot_ref[...] = w_ref[...] * rho * jnp.exp(jnp.log(1.0 + rho * rho) * (-1.0 / 3.0))
+    pot_ref[...] = w_ref[...].reshape(1, ROWS) * rho * jnp.exp(jnp.log(1.0 + rho * rho) * (-1.0 / 3.0))
 
     def weigh(c, carry):
         scaled_ref[c] = (
@@ -199,7 +221,6 @@
     lax.fori_loop(0, NCOL, weigh, 0)
 
     HALF = ENTRIES // 2
-    main_refs, far_refs = (main0_ref, main1_ref), (far0_ref, far1_ref)
 
     def return_round(n):
         rows = pl.ds(pl.multiple_of(n * RETURN_ROWS, RETURN_ROWS), RETURN_ROWS)
@@ -294,7 +315,7 @@
             rows = pl.ds(u * RUN, RUN)
 
             def add(m, acc):
-                acc = acc * keep_ref[which, m] + parts_ref[order_ref[m], rows, :].astype(jnp.float32)
+                acc = acc * keep_ref[which, m] + parts_ref[order_ref[0, m], rows, :].astype(jnp.float32)
                 run_ref[m] = acc
                 return acc
 
@@ -308,8 +329,8 @@
                     p = row + i * NROW
                     low = jnp.where(w == 1, p - 15, p - 15 + apart)
                     high = jnp.where(w == 1, p - 15 + apart, p + 1)
-                    before = below_ref[jnp.clip(low, 0, GROUPS)]
-                    until = below_ref[jnp.clip(high, 0, GROUPS)]
+                    before = below(jnp.clip(low, 0, GROUPS))
+                    until = below(jnp.clip(high, 0, GROUPS))
                     some = jnp.clip(until - before, 0, 1).astype(jnp.float32)
                     return run_ref[jnp.maximum(until - 1, 0)] * some
 
@@ -396,7 +417,7 @@
 HBM = pl.BlockSpec(memory_space=pl.ANY)
 
 
-def exchange(starts, order, below, cnt, w, dens, phi):
+def exchange(lists, home, cnt, w, dens, phi):
     sums = jax.ShapeDtypeStruct((SLOTS, B, B), jnp.float32)
     parts = (GROUPS, RETURN_ROWS, B)
     slots = (RETURN_ROUNDS, SLOTS, RETURN_ROWS, B)
@@ -404,7 +425,7 @@
     return pl.pallas_call(
         group_kernel,
         out_shape=[sums, sums, jax.ShapeDtypeStruct(slots, jnp.bfloat16)],
-        in_specs=[SMEM, SMEM, SMEM, SMEM, VMEM, HBM, HBM],
+        in_specs=[SMEM, SMEM, VMEM, VMEM, SMEM, VMEM, HBM, HBM],
         out_specs=[VMEM, VMEM, VMEM],
         scratch_shapes=[
             pltpu.VMEM((ENTRIES, BLOCK_ROWS, B, B), jnp.bfloat16),
@@ -416,69 +437,25 @@
             pltpu.VMEM((RETURN_ROUNDS, ENTRIES, ENTRIES, RETURN_ROWS, B), jnp.bfloat16),
             pltpu.VMEM((8, ROWS), jnp.float32),
             pltpu.VMEM((1, ROWS), jnp.float32),
-            pltpu.VMEM(parts, jnp.bfloat16),
-            pltpu.VMEM(parts, jnp.bfloat16),
-            pltpu.VMEM(parts, jnp.bfloat16),
-            pltpu.VMEM(parts, jnp.bfloat16),
+            [pltpu.VMEM(parts, jnp.bfloat16)] * RETURN_ROUNDS,
+            [pltpu.VMEM(parts, jnp.bfloat16)] * RETURN_ROUNDS,
             pltpu.VMEM((GROUPS, RUN, B), jnp.float32),
             pltpu.VMEM(slots, jnp.bfloat16),
             pltpu.VMEM(slots, jnp.bfloat16),
             pltpu.SMEM((2, GROUPS), jnp.float32),
-            dma, dma, dma, dma((GATHER_ROUNDS,)), dma, dma((RETURN_ROUNDS,)), dma, dma((RETURN_ROUNDS,)), dma,
+            pltpu.VMEM((8, GROUPS), jnp.int32),
+            pltpu.SMEM((8, GROUPS), jnp.int32),
+            dma, dma, dma, dma, dma((GATHER_ROUNDS,)), dma, dma((RETURN_ROUNDS,)), dma, dma((RETURN_ROUNDS,)), dma,
         ] + [dma((RETURN_ROUNDS, SLOTS))] * 4,
         compiler_params=pltpu.CompilerParams(
             collective_id=0, has_side_effects=True, vmem_limit_bytes=61 << 20
         ),
         cost_estimate=pl.CostEstimate(flops=4 * ROWS * WIDTH * WIDTH, bytes_accessed=16 << 20, transcendentals=2 * ROWS),
-    )(starts, order, below, cnt, w, dens, phi)
-
-
-def sort_kernel(list_ref, home_ref, start_ref, order_ref, below_ref, next_ref):
-    def clear(v, carry):
-        below_ref[v] = 0
-        return carry
-
-    def count(g, carry):
-        start = home_ref[list_ref[g, 0]]
-        start_ref[g] = start
-        below_ref[start + 1] += 1
-        return carry
-
-    def add(v, before):
-        before = before + below_ref[v]
-        below_ref[v] = before
-        next_ref[v] = before
-        return before
-
-    def put(g, carry):
-        start = start_ref[g]
-        at = next_ref[start]
-        order_ref[at] = g
-        next_ref[start] = at + 1
-        return carry
-
-    lax.fori_loop(0, GROUPS + 8, clear, 0, unroll=8)
-    lax.fori_loop(0, GROUPS, count, 0, unroll=8)
-    lax.fori_loop(0, GROUPS + 8, add, 0, unroll=8)
-    lax.fori_loop(0, GROUPS, put, 0, unroll=8)
-
-
-def sort_starts(lists, home):
-    return pl.pallas_call(
-        sort_kernel,
-        out_shape=[
-            jax.ShapeDtypeStruct((GROUPS,), jnp.int32),
-            jax.ShapeDtypeStruct((GROUPS,), jnp.int32),
-            jax.ShapeDtypeStruct((GROUPS + 8,), jnp.int32),
-        ],
-        in_specs=[SMEM, SMEM],
-        out_specs=[SMEM, SMEM, SMEM],
-        scratch_shapes=[pltpu.SMEM((GROUPS + 8,), jnp.int32)],
-    )(lists, home)
-
-
-def place_kernel(where_ref, near_ref, wide_ref, mirrored_ref, out_ref):
-    row, col = where_ref[0], where_ref[1]
+    )(lists, home, lists, home.reshape(1, GROUPS), cnt, w, dens, phi)
+
+
+def place_kernel(near_ref, wide_ref, mirrored_ref, out_ref):
+    row, col = lax.axis_index("row"), lax.axis_index("col")
     i = pl.program_id(0)
     shift = lag(row, col)
     out_ref[...] = jnp.zeros_like(out_ref)
@@ -489,38 +466,43 @@
 
     @pl.when(shift == 0)
     def _():
-        out_ref[:, columns(p)] = near_ref[i * 2]
+        out_ref[:, columns(p)] = near_ref[0]
         for w in range(2):
-            out_ref[:, columns(p + NCOL - NROW * w)] = wide_ref[i * 2 + w]
+            out_ref[:, columns(p + NCOL - NROW * w)] = wide_ref[w]
 
     @pl.when(shift != 0)
     def _():
         for w in range(2):
-            out_ref[:, columns(p + shift - NROW * w)] = near_ref[i * 2 + w]
+            out_ref[:, columns(p + shift - NROW * w)] = near_ref[w]
             there = p - (NCOL - shift) + NROW * w
             at = ((there & (GROUPS - 1)) >> 4) * 2 + w
             block = jnp.concatenate([mirrored_ref[n, at] for n in range(RETURN_ROUNDS)], axis=0)
             out_ref[:, columns(there)] = block.astype(jnp.float32).T
 
 
-def assemble(where, near, wide, mirrored):
+def assemble(near, wide, mirrored):
+    def wide_index(i):
+        return i * (lag(lax.axis_index("row"), lax.axis_index("col")) == 0).astype(jnp.int32), 0, 0
+
     return pl.pallas_call(
         place_kernel,
         grid=(BLOCK_ROWS,),
         out_shape=jax.ShapeDtypeStruct((BLOCK_ROWS * B, WIDTH), jnp.float32),
-        in_specs=[SMEM, VMEM, VMEM, VMEM],
+        in_specs=[
+            pl.BlockSpec((2, B, B), lambda i: (i, 0, 0)),
+            pl.BlockSpec((2, B, B), wide_index),
+            VMEM,
+        ],
         out_specs=pl.BlockSpec((B, WIDTH), lambda i: (i, 0)),
-    )(where, near, wide, mirrored)
+    )(near, wide, mirrored)
 
 
 def body(basis_values, point_weights, density_stored, relevant_blocks, relevant_count, block_home):
-    starts, order, below = sort_starts(relevant_blocks, block_home)
     near, wide, mirrored = exchange(
-        starts, order, below, relevant_count, point_weights.reshape(1, ROWS),
+        relevant_blocks.T, block_home, relevant_count, point_weights,
         density_stored.reshape(BLOCK_ROWS, B, WIDTH), basis_values,
     )
-    where = jnp.stack([lax.axis_index("row"), lax.axis_index("col")]).astype(jnp.int32)
-    return assemble(where, near, wide, mirrored)
+    return assemble(near, wide, mirrored)
 
 
 def solution(mesh):

time: 246 us -> 239 us (0.972)
  Pallas kernels: 242 us -> 239 us
  local copies, waits for them, and re-layouts: 2.72 us -> 0 us
    pallas_call x1 -> x0, Pallas kernels: 4.44 us -> none  [sort_starts(): pl.pallas_call(sort_kernel, out_shape=[jax.ShapeDtypeStruct((GROUPS,), jn...]
where the time goes in v4:
time: 239 us
  Pallas kernels  239 us (100%)
    pallas_call x1, Pallas kernels, exchange(): pl.pallas_call(group_kernel, out_shape=[sums, sums, jax.ShapeDtypeStruct(...  232 us
    pallas_call x1, Pallas kernels, assemble(): pl.pallas_call(place_kernel, grid=(BLOCK_ROWS,), out_shape=jax.ShapeDtype...  7.23 us

profile of v4, /device:TPU:0, one launch (start us, length us, event | category | flops | bytes accessed | tf_op | source)
XLA Modules:
  0.0 238.9 jit_solution(17007576820073503754)
XLA Ops:
  0.0 231.6 %shard_map.64 = (f32[16,128,128]{2,1,0:T(8,128)}, f32[16,128,128]{2,1,0:T(8,128)}, bf16[2,16,64,128]{3,2,1,0:T(8,128)(2,1)}) custom-call(s32[16,128]{1,0:T(8,128)} %bitcast.4, s32[128]{0:T(128)} %home_ref.1, s32[16,128]{1,0:T(8,128)} %bitcast.5, s32[1,128]{1,0:T(1,128)} %bitcast.6, s32[128]{0:T(128)} %cnt_ref.1, f32[1536]{0:T(1024)} %w_ref.1, ...), custom_call_target="tpu_custom_call" | custom-call | flops 25769803776 | bytes 16777216 | tf_op jit(solution)/shard_map/pallas_call | solution.py:425
  231.6 7.2 %shard_map.65 = f32[1024,2048]{1,0:T(8,128)} custom-call(f32[16,128,128]{2,1,0:T(8,128)} %get-tuple-element.8.near_ref, f32[16,128,128]{2,1,0:T(8,128)} %get-tuple-element.9.wide_ref, bf16[2,16,64,128]{3,2,1,0:T(8,128)(2,1)} %get-tuple-element.10.mirrored_ref), custom_call_target="tpu_custom_call" | custom-call | tf_op jit(solution)/shard_map/pallas_call | solution.py:487

commit v5 on v4

--- a/solution.py
+++ b/solution.py
@@ -40,6 +40,10 @@
 
 def lag(row, col):
     return (col - row + NROW) % NCOL
+
+
+def keeps_far(row, col):
+    return (lag(row, col) == 0) & (row < NCOL)
 
 
 def mirror_owner(row, col):
@@ -259,7 +263,7 @@
             r, c = offset_target(i, row, col)
             main_copy(r, c).start()
 
-            @pl.when(lag(r, c) == 0)
+            @pl.when(keeps_far(r, c))
             def _():
                 far_copy(r, c).start()
 
@@ -271,7 +275,7 @@
         own.start()
         own.wait()
 
-        @pl.when(lag(row, col) == 0)
+        @pl.when(keeps_far(row, col))
         def _():
             residue = (row + NCOL) % NROW
             own = pltpu.make_async_copy(back_ref.at[n, place(residue), place(row)], far_refs[n].at[me], self_sem)
@@ -350,19 +354,27 @@
         pltpu.make_async_copy(one_part, one_part, mrecv.at[n]).wait()
         total(main_refs[n], n, 0, shift, near_ref)
 
-        def start_first(i, carry):
-            rows = pl.ds(pl.multiple_of(n * RETURN_ROWS, RETURN_ROWS), RETURN_ROWS)
-            turned_ref[n, i] = near_ref[i, rows, :].astype(jnp.bfloat16)
-            first(n, i).start()
-            return carry
-
-        lax.fori_loop(0, SLOTS, start_first, 0)
-
-        @pl.when(shift == 0)
+        @pl.when(keeps_far(row, col))
         def _():
             pltpu.make_async_copy(one_part, one_part, frecv.at[n]).wait()
             total(far_refs[n], n, 1, NCOL, wide_ref)
 
+        def start_first(i, carry):
+            rows = pl.ds(pl.multiple_of(n * RETURN_ROWS, RETURN_ROWS), RETURN_ROWS)
+
+            @pl.when(keeps_far(row, col))
+            def _():
+                turned_ref[n, i] = wide_ref[i, rows, :].astype(jnp.bfloat16)
+
+            @pl.when(jnp.logical_not(keeps_far(row, col)))
+            def _():
+                turned_ref[n, i] = near_ref[i, rows, :].astype(jnp.bfloat16)
+
+            first(n, i).start()
+            return carry
+
+        lax.fori_loop(0, SLOTS, start_first, 0)
+
         def pass_on(i, carry):
             first(n, i).wait_recv()
 
@@ -378,7 +390,7 @@
 
         lax.fori_loop(0, SLOTS, pass_on, 0)
 
-    @pl.when(shift != 0)
+    @pl.when(jnp.logical_not(keeps_far(row, col)))
     def _():
         wide_ref[...] = jnp.zeros_like(wide_ref)
 
@@ -401,14 +413,14 @@
     sent = stage_ref.at[pl.ds(0, (GROUPS - 1) * B // 2)]
     pltpu.make_async_copy(sent, sent, msend).wait()
 
-    @pl.when(shift == 0)
-    def _():
-        others = stage_ref.at[pl.ds(0, (NROW - 1) * B // 2)]
+    @pl.when(keeps_far(row, col))
+    def _():
+        others = stage_ref.at[pl.ds(0, (NCOL - 1) * B // 2)]
         pltpu.make_async_copy(others, others, fsend).wait()
 
-    @pl.when(shift != 0)
-    def _():
-        others = stage_ref.at[pl.ds(0, NROW * B // 2)]
+    @pl.when(jnp.logical_not(keeps_far(row, col)))
+    def _():
+        others = stage_ref.at[pl.ds(0, NCOL * B // 2)]
         pltpu.make_async_copy(others, others, fsend).wait()
 
 
@@ -467,13 +479,20 @@
     @pl.when(shift == 0)
     def _():
         out_ref[:, columns(p)] = near_ref[0]
+
+    @pl.when(shift != 0)
+    def _():
+        for w in range(2):
+            out_ref[:, columns(p + shift - NROW * w)] = near_ref[w]
+
+    @pl.when(keeps_far(row, col))
+    def _():
         for w in range(2):
             out_ref[:, columns(p + NCOL - NROW * w)] = wide_ref[w]
 
-    @pl.when(shift != 0)
+    @pl.when(jnp.logical_not(keeps_far(row, col)))
     def _():
         for w in range(2):
-            out_ref[:, columns(p + shift - NROW * w)] = near_ref[w]
             there = p - (NCOL - shift) + NROW * w
             at = ((there & (GROUPS - 1)) >> 4) * 2 + w
             block = jnp.concatenate([mirrored_ref[n, at] for n in range(RETURN_ROUNDS)], axis=0)
@@ -482,7 +501,7 @@
 
 def assemble(near, wide, mirrored):
     def wide_index(i):
-        return i * (lag(lax.axis_index("row"), lax.axis_index("col")) == 0).astype(jnp.int32), 0, 0
+        return i * keeps_far(lax.axis_index("row"), lax.axis_index("col")).astype(jnp.int32), 0, 0
 
     return pl.pallas_call(
         place_kernel,

time: 239 us -> 242 us (1.013)
  Pallas kernels: 239 us -> 242 us
    pallas_call x1, Pallas kernels: 232 us -> 235 us  [exchange(): pl.pallas_call(group_kernel, out_shape=[sums, sums, jax.ShapeDtypeStruct(...]
where the time goes in v5:
time: 242 us
  Pallas kernels  242 us (100%)
    pallas_call x1, Pallas kernels, exchange(): pl.pallas_call(group_kernel, out_shape=[sums, sums, jax.ShapeDtypeStruct(...  235 us
    pallas_call x1, Pallas kernels, assemble(): pl.pallas_call(place_kernel, grid=(BLOCK_ROWS,), out_shape=jax.ShapeDtype...  7.25 us

profile of v5, /device:TPU:0, one launch (start us, length us, event | category | flops | bytes accessed | tf_op | source)
XLA Modules:
  0.0 241.9 jit_solution(11686812773019830563)
XLA Ops:
  0.0 234.6 %shard_map.64 = (f32[16,128,128]{2,1,0:T(8,128)}, f32[16,128,128]{2,1,0:T(8,128)}, bf16[2,16,64,128]{3,2,1,0:T(8,128)(2,1)}) custom-call(s32[16,128]{1,0:T(8,128)} %bitcast.4, s32[128]{0:T(128)} %home_ref.1, s32[16,128]{1,0:T(8,128)} %bitcast.5, s32[1,128]{1,0:T(1,128)} %bitcast.6, s32[128]{0:T(128)} %cnt_ref.1, f32[1536]{0:T(1024)} %w_ref.1, ...), custom_call_target="tpu_custom_call" | custom-call | flops 25769803776 | bytes 16777216 | tf_op jit(solution)/shard_map/pallas_call | solution.py:437
  234.6 7.2 %shard_map.65 = f32[1024,2048]{1,0:T(8,128)} custom-call(f32[16,128,128]{2,1,0:T(8,128)} %get-tuple-element.8.near_ref, f32[16,128,128]{2,1,0:T(8,128)} %get-tuple-element.9.wide_ref, bf16[2,16,64,128]{3,2,1,0:T(8,128)(2,1)} %get-tuple-element.10.mirrored_ref), custom_call_target="tpu_custom_call" | custom-call | tf_op jit(solution)/shard_map/pallas_call | solution.py:506

commit v6 on v5

--- a/solution.py
+++ b/solution.py
@@ -11,7 +11,7 @@
 ROWS = 1536
 WIDTH = ENTRIES * B
 BLOCK_ROWS = 8
-GATHER_ROUNDS, GATHER_ROWS = 4, 32
+GATHER_ROUNDS, GATHER_ROWS = 8, 16
 RETURN_ROUNDS, RETURN_ROWS = 2, 64
 RUN = 32
 SLOTS = 2 * BLOCK_ROWS
@@ -323,7 +323,7 @@
                 run_ref[m] = acc
                 return acc
 
-            lax.fori_loop(0, GROUPS, add, jnp.zeros((RUN, B), jnp.float32))
+            lax.fori_loop(0, GROUPS, add, jnp.zeros((RUN, B), jnp.float32), unroll=8)
             out_rows = pl.ds(pl.multiple_of(n * RETURN_ROWS + u * RUN, RUN), RUN)
 
             def slot(at, carry):
@@ -351,8 +351,11 @@
     one_part = stage_ref.at[pl.ds(0, (GROUPS - 1) * RETURN_ROWS // 2)]
 
     def finish_round(n):
-        pltpu.make_async_copy(one_part, one_part, mrecv.at[n]).wait()
-        total(main_refs[n], n, 0, shift, near_ref)
+        def total_near():
+            pltpu.make_async_copy(one_part, one_part, mrecv.at[n]).wait()
+            total(main_refs[n], n, 0, shift, near_ref)
+
+        pl.when(jnp.logical_not(keeps_far(row, col)))(total_near)
 
         @pl.when(keeps_far(row, col))
         def _():
@@ -389,6 +392,7 @@
             return carry
 
         lax.fori_loop(0, SLOTS, pass_on, 0)
+        pl.when(keeps_far(row, col))(total_near)
 
     @pl.when(jnp.logical_not(keeps_far(row, col)))
     def _():
@@ -466,54 +470,82 @@
     )(lists, home, lists, home.reshape(1, GROUPS), cnt, w, dens, phi)
 
 
-def place_kernel(near_ref, wide_ref, mirrored_ref, out_ref):
+def place_kernel(near_hbm, wide_hbm, mirrored_hbm, out_hbm, near_ref, wide_ref, mirrored_ref, rows_ref, in_sem, out_sem):
     row, col = lax.axis_index("row"), lax.axis_index("col")
-    i = pl.program_id(0)
     shift = lag(row, col)
-    out_ref[...] = jnp.zeros_like(out_ref)
-    p = row + NROW * i
+    near_copy = pltpu.make_async_copy(near_hbm, near_ref, in_sem.at[0])
+    wide_copy = pltpu.make_async_copy(wide_hbm, wide_ref, in_sem.at[1])
+    mirrored_copy = pltpu.make_async_copy(mirrored_hbm, mirrored_ref, in_sem.at[2])
+    for copy in (near_copy, wide_copy, mirrored_copy):
+        copy.start()
+
+    def clear(i, carry):
+        rows_ref[i] = jnp.zeros((B, WIDTH), jnp.float32)
+        return carry
+
+    lax.fori_loop(0, BLOCK_ROWS, clear, 0)
+    for copy in (near_copy, wide_copy, mirrored_copy):
+        copy.wait()
 
     def columns(q):
         return pl.ds(pl.multiple_of(((q & (GROUPS - 1)) >> 3) * B, B), B)
 
-    @pl.when(shift == 0)
-    def _():
-        out_ref[:, columns(p)] = near_ref[0]
-
-    @pl.when(shift != 0)
-    def _():
-        for w in range(2):
-            out_ref[:, columns(p + shift - NROW * w)] = near_ref[w]
-
-    @pl.when(keeps_far(row, col))
-    def _():
-        for w in range(2):
-            out_ref[:, columns(p + NCOL - NROW * w)] = wide_ref[w]
-
-    @pl.when(jnp.logical_not(keeps_far(row, col)))
-    def _():
-        for w in range(2):
-            there = p - (NCOL - shift) + NROW * w
-            at = ((there & (GROUPS - 1)) >> 4) * 2 + w
-            block = jnp.concatenate([mirrored_ref[n, at] for n in range(RETURN_ROUNDS)], axis=0)
-            out_ref[:, columns(there)] = block.astype(jnp.float32).T
+    def out_copy(i):
+        return pltpu.make_async_copy(rows_ref.at[i], out_hbm.at[i], out_sem.at[i])
+
+    def fill(i, carry):
+        p = row + NROW * i
+
+        @pl.when(shift == 0)
+        def _():
+            rows_ref[i, :, columns(p)] = near_ref[i * 2]
+
+        @pl.when(shift != 0)
+        def _():
+            for w in range(2):
+                rows_ref[i, :, columns(p + shift - NROW * w)] = near_ref[i * 2 + w]
+
+        @pl.when(keeps_far(row, col))
+        def _():
+            for w in range(2):
+                rows_ref[i, :, columns(p + NCOL - NROW * w)] = wide_ref[i * 2 + w]
+
+        @pl.when(jnp.logical_not(keeps_far(row, col)))
+        def _():
+            for w in range(2):
+                there = p - (NCOL - shift) + NROW * w
+                at = ((there & (GROUPS - 1)) >> 4) * 2 + w
+                block = jnp.concatenate([mirrored_ref[n, at] for n in range(RETURN_ROUNDS)], axis=0)
+                rows_ref[i, :, columns(there)] = block.astype(jnp.float32).T
+
+        out_copy(i).start()
+        return carry
+
+    lax.fori_loop(0, BLOCK_ROWS, fill, 0)
+
+    def drain(i, carry):
+        out_copy(i).wait()
+        return carry
+
+    lax.fori_loop(0, BLOCK_ROWS, drain, 0)
 
 
 def assemble(near, wide, mirrored):
-    def wide_index(i):
-        return i * keeps_far(lax.axis_index("row"), lax.axis_index("col")).astype(jnp.int32), 0, 0
-
     return pl.pallas_call(
         place_kernel,
-        grid=(BLOCK_ROWS,),
-        out_shape=jax.ShapeDtypeStruct((BLOCK_ROWS * B, WIDTH), jnp.float32),
-        in_specs=[
-            pl.BlockSpec((2, B, B), lambda i: (i, 0, 0)),
-            pl.BlockSpec((2, B, B), wide_index),
-            VMEM,
+        out_shape=jax.ShapeDtypeStruct((BLOCK_ROWS, B, WIDTH), jnp.float32),
+        in_specs=[HBM] * 3,
+        out_specs=HBM,
+        scratch_shapes=[
+            pltpu.VMEM((SLOTS, B, B), jnp.float32),
+            pltpu.VMEM((SLOTS, B, B), jnp.float32),
+            pltpu.VMEM((RETURN_ROUNDS, SLOTS, RETURN_ROWS, B), jnp.bfloat16),
+            pltpu.VMEM((BLOCK_ROWS, B, WIDTH), jnp.float32),
+            pltpu.SemaphoreType.DMA((3,)),
+            pltpu.SemaphoreType.DMA((BLOCK_ROWS,)),
         ],
-        out_specs=pl.BlockSpec((B, WIDTH), lambda i: (i, 0)),
-    )(near, wide, mirrored)
+        compiler_params=pltpu.CompilerParams(vmem_limit_bytes=32 << 20),
+    )(near, wide, mirrored).reshape(BLOCK_ROWS * B, WIDTH)
 
 
 def body(basis_values, point_weights, density_stored, relevant_blocks, relevant_count, block_home):

time: 242 us -> 239 us (0.988)
  Pallas kernels: 242 us -> 235 us
  local copies, waits for them, and re-layouts: 0 us -> 3.48 us
    pallas_call x1, Pallas kernels: 235 us -> 231 us  [exchange(): pl.pallas_call(group_kernel, out_shape=[sums, sums, jax.ShapeDtypeStruct(...]
    unnamed x0 -> x6, local copies, waits for them, and re-layouts: none -> 3.48 us
    pallas_call x1, Pallas kernels: 7.25 us -> 4.15 us  [assemble(): pl.pallas_call(place_kernel, out_shape=jax.ShapeDtypeStruct((BLOCK_ROWS,...]
where the time goes in v6:
time: 239 us; the launch traced here: 238 us
  Pallas kernels  235 us (98%)
  local copies, waits for them, and re-layouts  3.48 us (1%)
    pallas_call x1, Pallas kernels, exchange(): pl.pallas_call(group_kernel, out_shape=[sums, sums, jax.ShapeDtypeStruct(...  231 us

profile of v6, /device:TPU:0, one launch (start us, length us, event | category | flops | bytes accessed | tf_op | source)
XLA Modules:
  0.0 238.3 jit_solution(16892706892630935863)
XLA Ops:
  0.0 230.7 %shard_map.64 = (f32[16,128,128]{2,1,0:T(8,128)}, f32[16,128,128]{2,1,0:T(8,128)}, bf16[2,16,64,128]{3,2,1,0:T(8,128)(2,1)}) custom-call(s32[16,128]{1,0:T(8,128)} %bitcast.5, s32[128]{0:T(128)} %home_ref.1, s32[16,128]{1,0:T(8,128)} %bitcast.6, s32[1,128]{1,0:T(1,128)} %bitcast.7, s32[128]{0:T(128)} %cnt_ref.1, f32[1536]{0:T(1024)} %w_ref.1, ...), custom_call_target="tpu_custom_call" | custom-call | flops 25769803776 | bytes 16777216 | tf_op jit(solution)/shard_map/pallas_call | solution.py:441
  230.7 0.0 copy-start
  230.7 1.2 copy-done
  231.9 0.0 copy-start.1
  231.9 1.2 copy-done.1
  233.1 0.0 copy-start.2
  233.1 1.0 copy-done.2
  234.2 4.1 %shard_map.65 = f32[8,128,2048]{2,1,0:T(8,128)} custom-call(f32[16,128,128]{2,1,0:T(8,128)S(1)} %copy-done, f32[16,128,128]{2,1,0:T(8,128)S(1)} %copy-done.1, bf16[2,16,64,128]{3,2,1,0:T(8,128)(2,1)S(1)} %copy-done.2), custom_call_target="tpu_custom_call" | custom-call | tf_op jit(solution)/shard_map/pallas_call | solution.py:534
Async XLA Ops:
  230.7 1.2 copy-start
  231.9 1.2 copy-start.1
  233.1 1.0 copy-start.2

commit v7 on v6

--- a/solution.py
+++ b/solution.py
@@ -544,7 +544,7 @@
             pltpu.SemaphoreType.DMA((3,)),
             pltpu.SemaphoreType.DMA((BLOCK_ROWS,)),
         ],
-        compiler_params=pltpu.CompilerParams(vmem_limit_bytes=32 << 20),
+        compiler_params=pltpu.CompilerParams(vmem_limit_bytes=62 << 20),
     )(near, wide, mirrored).reshape(BLOCK_ROWS * B, WIDTH)
 
 

time: 239 us -> 236 us (0.987)
  local copies, waits for them, and re-layouts: 3.48 us -> 0 us
    unnamed x6 -> x0, local copies, waits for them, and re-layouts: 3.48 us -> none
where the time goes in v7:
time: 236 us
  Pallas kernels  236 us (100%)
    pallas_call x1, Pallas kernels, exchange(): pl.pallas_call(group_kernel, out_shape=[sums, sums, jax.ShapeDtypeStruct(...  231 us
    pallas_call x1, Pallas kernels, assemble(): pl.pallas_call(place_kernel, out_shape=jax.ShapeDtypeStruct((BLOCK_ROWS,...  5.09 us

profile of v7, /device:TPU:0, one launch (start us, length us, event | category | flops | bytes accessed | tf_op | source)
XLA Modules:
  0.0 235.8 jit_solution(10732389478214270607)
XLA Ops:
  0.0 230.7 %shard_map.64 = (f32[16,128,128]{2,1,0:T(8,128)}, f32[16,128,128]{2,1,0:T(8,128)}, bf16[2,16,64,128]{3,2,1,0:T(8,128)(2,1)}) custom-call(s32[16,128]{1,0:T(8,128)} %bitcast.5, s32[128]{0:T(128)} %home_ref.1, s32[16,128]{1,0:T(8,128)} %bitcast.6, s32[1,128]{1,0:T(1,128)} %bitcast.7, s32[128]{0:T(128)} %cnt_ref.1, f32[1536]{0:T(1024)} %w_ref.1, ...), custom_call_target="tpu_custom_call" | custom-call | flops 25769803776 | bytes 16777216 | tf_op jit(solution)/shard_map/pallas_call | solution.py:441
  230.7 5.1 %shard_map.65 = f32[8,128,2048]{2,1,0:T(8,128)} custom-call(f32[16,128,128]{2,1,0:T(8,128)} %get-tuple-element.8.near_hbm, f32[16,128,128]{2,1,0:T(8,128)} %get-tuple-element.9.wide_hbm, bf16[2,16,64,128]{3,2,1,0:T(8,128)(2,1)} %get-tuple-element.10.mirrored_hbm), custom_call_target="tpu_custom_call" | custom-call | tf_op jit(solution)/shard_map/pallas_call | solution.py:534

commit v8 on v7

--- a/solution.py
+++ b/solution.py
@@ -111,7 +111,7 @@
             stage_ref[staged(n, r, c), pl.ds(B, B)] = right[part]
         return carry
 
-    lax.fori_loop(1, GROUPS, prepare, 0)
+    lax.fori_loop(1, GROUPS, prepare, 0, unroll=2)
     my_rows = pl.ds(pl.multiple_of(place(row) * GATHER_ROWS, GATHER_ROWS), GATHER_ROWS)
     my_cols = pl.ds(pl.multiple_of(col * 2 * B, B), 2 * B)
     left, right = pick(row, col)
@@ -132,7 +132,7 @@
             ).start()
             return carry
 
-        return lax.fori_loop(1, GROUPS, send, carry)
+        return lax.fori_loop(1, GROUPS, send, carry, unroll=2)
 
     lax.fori_loop(0, GATHER_ROUNDS, send_round, 0)
 
@@ -269,7 +269,7 @@
 
             return carry
 
-        lax.fori_loop(1, GROUPS, give, 0)
+        lax.fori_loop(1, GROUPS, give, 0, unroll=2)
         residue = (row + lag(row, col)) % NROW
         own = pltpu.make_async_copy(back_ref.at[n, place(residue), place(row)], main_refs[n].at[me], self_sem)
         own.start()

time: 236 us -> 234 us (level)
  no operation moved by 1% of the time
where the time goes in v8:
time: 234 us
  Pallas kernels  234 us (100%)
    pallas_call x1, Pallas kernels, exchange(): pl.pallas_call(group_kernel, out_shape=[sums, sums, jax.ShapeDtypeStruct(...  229 us
    pallas_call x1, Pallas kernels, assemble(): pl.pallas_call(place_kernel, out_shape=jax.ShapeDtypeStruct((BLOCK_ROWS,...  5.09 us

profile of v8, /device:TPU:0, one launch (start us, length us, event | category | flops | bytes accessed | tf_op | source)
XLA Modules:
  0.0 234.3 jit_solution(9194545272231304221)
XLA Ops:
  0.0 229.2 %shard_map.64 = (f32[16,128,128]{2,1,0:T(8,128)}, f32[16,128,128]{2,1,0:T(8,128)}, bf16[2,16,64,128]{3,2,1,0:T(8,128)(2,1)}) custom-call(s32[16,128]{1,0:T(8,128)} %bitcast.5, s32[128]{0:T(128)} %home_ref.1, s32[16,128]{1,0:T(8,128)} %bitcast.6, s32[1,128]{1,0:T(1,128)} %bitcast.7, s32[128]{0:T(128)} %cnt_ref.1, f32[1536]{0:T(1024)} %w_ref.1, ...), custom_call_target="tpu_custom_call" | custom-call | flops 25769803776 | bytes 16777216 | tf_op jit(solution)/shard_map/pallas_call | solution.py:441
  229.2 5.1 %shard_map.65 = f32[8,128,2048]{2,1,0:T(8,128)} custom-call(f32[16,128,128]{2,1,0:T(8,128)} %get-tuple-element.8.near_hbm, f32[16,128,128]{2,1,0:T(8,128)} %get-tuple-element.9.wide_hbm, bf16[2,16,64,128]{3,2,1,0:T(8,128)(2,1)} %get-tuple-element.10.mirrored_hbm), custom_call_target="tpu_custom_call" | custom-call | tf_op jit(solution)/shard_map/pallas_call | solution.py:534
